TPU v7x, 512 devices: a whole 4x8x8 slice. The times are simulated.
512 devices in a mesh: gx: 16 (over z_hi, y), gy: 32 (over z_lo, x, core).
Axes of the slice: x: 4, y: 8, z: 8 (z_hi: 2, z_lo: 4; z = z_hi * 4 + z_lo), core: 2. Of those that a mesh axis runs over, the one named last changes fastest.
Arguments:
- intensities: int32 [384, 256, 128], P('gx', 'gy'), may hold values from 0 to 255
- labels: int32 [384, 256, 128], P('gx', 'gy'), may hold values from 0 to 2
Outputs:
- solution: float32 [384, 256, 128], P('gx', 'gy')
All inputs are finite; a program needn't handle non-finite values.
Results may differ from a plain program's by a relative error of at most 0.0001.
Values sent between devices are 32-bit elements; how exact they have to be, the bound alone decides.
A program may use at most 64 MiB of HBM per device.

v0:
```python
import jax
import jax.numpy as jnp
from jax import lax
from jax.sharding import PartitionSpec as P

COARSE_ITERS = 30


edge_beta = 3.0
seed_gamma = 4.0
base_mass = 0.1
damping = 0.7


def with_halo(block, sides, width):
    for axis, dim in sides:
        count = lax.axis_size(axis)
        forward = [(i, i + 1) for i in range(count - 1)]
        backward = [(target, source) for source, target in forward]
        low = lax.ppermute(
            lax.slice_in_dim(block, block.shape[dim] - width, None, axis=dim), axis, forward
        )
        high = lax.ppermute(lax.slice_in_dim(block, 0, width, axis=dim), axis, backward)
        block = jnp.concatenate([low, block, high], axis=dim)
    return block


def edge_weight(upper, lower):
    scaled = (upper - lower) / 255.0
    return jnp.exp(-edge_beta * scaled * scaled)


def pad_axis(array, axis, before, after):
    widths = [(0, 0), (0, 0), (0, 0)]
    widths[axis] = (before, after)
    return jnp.pad(array, widths)


def coarsen_operator(operator):
    plus_x, minus_x, plus_y, minus_y, plus_z, minus_z, mass_term = operator

    def blocks(array):
        size_a, size_b, size_c = array.shape
        return array.reshape(size_a // 2, 2, size_b // 2, 2, size_c // 2, 2)

    return (
        blocks(plus_x)[:, 1].sum(axis=(2, 4)),
        blocks(minus_x)[:, 0].sum(axis=(2, 4)),
        blocks(plus_y)[:, :, :, 1].sum(axis=(1, 4)),
        blocks(minus_y)[:, :, :, 0].sum(axis=(1, 4)),
        blocks(plus_z)[:, :, :, :, :, 1].sum(axis=(1, 3)),
        blocks(minus_z)[:, :, :, :, :, 0].sum(axis=(1, 3)),
        blocks(mass_term).sum(axis=(1, 3, 5)),
    )


def restrict_field(field):
    size_a, size_b, size_c = field.shape
    return field.reshape(size_a // 2, 2, size_b // 2, 2, size_c // 2, 2).sum(axis=(1, 3, 5))


def prolong_field(field):
    size_a, size_b, size_c = field.shape
    spread = jnp.broadcast_to(field[:, None, :, None, :, None], (size_a, 2, size_b, 2, size_c, 2))
    return spread.reshape(size_a * 2, size_b * 2, size_c * 2)


def diagonal_of(operator):
    plus_x, minus_x, plus_y, minus_y, plus_z, minus_z, mass_term = operator
    return mass_term + plus_x + minus_x + plus_y + minus_y + plus_z + minus_z


def apply_operator(padded, operator):
    plus_x, minus_x, plus_y, minus_y, plus_z, minus_z, mass_term = operator
    center = padded[1:-1, 1:-1]
    zpadded = jnp.pad(center, ((0, 0), (0, 0), (1, 1)))
    result = mass_term * center
    result = result + plus_x * (center - padded[2:, 1:-1]) + minus_x * (center - padded[:-2, 1:-1])
    result = result + plus_y * (center - padded[1:-1, 2:]) + minus_y * (center - padded[1:-1, :-2])
    result = (
        result + plus_z * (center - zpadded[:, :, 2:]) + minus_z * (center - zpadded[:, :, :-2])
    )
    return result


def relax(field, padded, rhs, operator, diagonal):
    return field + damping * (rhs - apply_operator(padded, operator)) / diagonal


def smooth_halo(field):
    return with_halo(field, (("gx", 0), ("gy", 1)), 1)


def fine_operator(intensities, labels):
    rimmed = with_halo(intensities, (("gx", 0), ("gy", 1)), 1).astype(jnp.float32)
    count_x, count_y, count_z = intensities.shape
    center = rimmed[1:-1, 1:-1]
    total_x = count_x * lax.axis_size("gx")
    total_y = count_y * lax.axis_size("gy")
    places_x = lax.axis_index("gx") * count_x + lax.broadcasted_iota(jnp.int32, center.shape, 0)
    places_y = lax.axis_index("gy") * count_y + lax.broadcasted_iota(jnp.int32, center.shape, 1)
    plus_x = jnp.where(places_x == total_x - 1, 0.0, edge_weight(rimmed[2:, 1:-1], center))
    minus_x = jnp.where(places_x == 0, 0.0, edge_weight(center, rimmed[:-2, 1:-1]))
    plus_y = jnp.where(places_y == total_y - 1, 0.0, edge_weight(rimmed[1:-1, 2:], center))
    minus_y = jnp.where(places_y == 0, 0.0, edge_weight(center, rimmed[1:-1, :-2]))
    weights_z = edge_weight(center[:, :, 1:], center[:, :, :-1])
    plus_z = pad_axis(weights_z, 2, 0, 1)
    minus_z = pad_axis(weights_z, 2, 1, 0)
    mass_term = (base_mass + jnp.where(labels > 0, seed_gamma, 0.0)).astype(jnp.float32)
    rhs = jnp.where(labels == 1, seed_gamma, 0.0).astype(jnp.float32)
    return ((plus_x, minus_x, plus_y, minus_y, plus_z, minus_z, mass_term), rhs)


def shards(intensities, labels):
    operator, rhs = fine_operator(intensities, labels)
    operators = [operator]
    for level in range(3):
        operators.append(coarsen_operator(operators[-1]))
    coarsest = operators[3]

    def coarse_solve(source):
        diagonal = diagonal_of(coarsest)

        def spread_turn(index, state):
            padded = with_halo(state, (("gx", 0), ("gy", 1)), 1)
            return relax(state, padded, source, coarsest, diagonal)

        return lax.fori_loop(1, COARSE_ITERS, spread_turn, damping * source / diagonal)

    def cycle(level, source):
        if level == 3:
            return coarse_solve(source)
        current = operators[level]
        diagonal = diagonal_of(current)
        field = damping * source / diagonal
        field = relax(field, smooth_halo(field), source, current, diagonal)
        residual = source - apply_operator(smooth_halo(field), current)
        field = field + prolong_field(cycle(level + 1, restrict_field(residual)))
        field = relax(field, smooth_halo(field), source, current, diagonal)
        field = relax(field, smooth_halo(field), source, current, diagonal)
        return field

    return cycle(0, rhs)


def solution(mesh):
    return jax.shard_map(
        shards,
        mesh=mesh,
        in_specs=(P("gx", "gy", None), P("gx", "gy", None)),
        out_specs=P("gx", "gy", None),
        check_vma=False,
    )
```

profile of v0, /device:TPU:63, one launch (start us, length us, event | category | flops | bytes accessed | tf_op | source)
XLA Modules:
  0.0 1062.6 jit_solution(13776795705862687250)
XLA Ops:
  0.7 9.8 collective-permute-start.4
  33.3 9.4 collective-permute-start.9
  42.7 7.6 reshape.185
  53.6 7.6 reshape.184
  66.1 7.6 reshape.183
  76.1 7.6 reshape.182
  86.2 7.6 reshape.181
  96.2 7.6 reshape.180
  123.5 9.4 collective-permute-start.13
  138.8 7.6 reshape.179
  150.7 7.6 reshape.178
  163.6 9.9 collective-permute-start.17
  190.0 9.9 collective-permute-start.21
  213.5 9.9 collective-permute-start.25
  236.1 9.9 collective-permute-start.29
  256.9 659.4 %while.12 = (s32[]{:T(128)}, f32[3,1,16]{2,1,0:T(1,128)S(1)}, f32[3,1,16]{2,1,0:T(1,128)S(1)}, f32[3,1,16]{2,1,0:T(1,128)S(1)}, f32[3,1,16]{2,1,0:T(1,128)S(1)},...) while((s32[]{:T(128)}, f32[3,1,16]{2,1,0:T(1,128)S(1)}, ...), condition=%wide.region_29.30_spmd, body=%wide.region_28.29_spmd.sunk | while | flops 1202 | bytes 11285 | solution.py:128
  256.9 9.9 collective-permute-start
  268.8 8.3 collective-permute-done.1
  293.0 6.9 collective-permute-done.1
  315.4 6.9 collective-permute-done.1
  337.9 6.9 collective-permute-done.1
  360.3 6.9 collective-permute-done.1
  382.8 6.9 collective-permute-done.1
  405.2 6.9 collective-permute-done.1
  427.7 6.9 collective-permute-done.1
  674.7 6.9 collective-permute-done.1
  918.4 9.4 collective-permute-start.33
  940.9 9.9 collective-permute-start.37
  964.1 9.9 collective-permute-start.41
  986.6 9.9 collective-permute-start.45
  1018.4 9.9 collective-permute-start.49
  1041.1 9.9 collective-permute-start.53
  (605 shorter events, 797.8 us)
Async XLA Ops:
  0.7 12.7 %collective-permute-start.4 = (s32[1,8,128]{2,1,0:T(8,128)S(1)}, s32[1,8,128]{2,1,0:T(8,128)S(1)}, u32[]{:S(2)}, u32[]{:S(2)}) collective-permute-start(s32[1,8,128]{2,1,0:T(8,128)S(1)} %get-tuple-element.220), channel_id=1, source_target_pairs={{0,32},{32,64},{64,96},{96,128},{128,160},{160,192},{192,224},{224... | collective-permute-start | bytes 12296 | tf_op jit(solution)/shard_map/ppermute | solution.py:20
  10.5 10.4 collective-permute-start.5
  31.4 76.6 %collective-permute-start.8 = (f32[1,8,128]{2,1,0:T(8,128)S(1)}, f32[1,8,128]{2,1,0:T(8,128)S(1)}, u32[]{:S(2)}, u32[]{:S(2)}) collective-permute-start(f32[1,8,128]{2,1,0:T(8,128)S(1)} %get-tuple-element.218), channel_id=1, source_target_pairs={{32,0},{64,32},{96,64},{128,96},{160,128},{192,160},{224,192},{256... | collective-permute-start | bytes 12296 | tf_op jit(solution)/shard_map/ppermute | solution.py:23
  33.3 74.7 %collective-permute-start.9 = (f32[1,8,128]{2,1,0:T(8,128)S(1)}, f32[1,8,128]{2,1,0:T(8,128)S(1)}, u32[]{:S(2)}, u32[]{:S(2)}) collective-permute-start(f32[1,8,128]{2,1,0:T(8,128)S(1)} %get-tuple-element.217), channel_id=1, source_target_pairs={{0,32},{32,64},{64,96},{96,128},{128,160},{160,192},{192,224},{224... | collective-permute-start | bytes 12296 | tf_op jit(solution)/shard_map/ppermute | solution.py:20
  121.6 12.3 %collective-permute-start.12 = (f32[1,8,128]{2,1,0:T(8,128)S(1)}, f32[1,8,128]{2,1,0:T(8,128)S(1)}, u32[]{:S(2)}, u32[]{:S(2)}) collective-permute-start(f32[1,8,128]{2,1,0:T(8,128)S(1)} %get-tuple-element.214), channel_id=1, source_target_pairs={{32,0},{64,32},{96,64},{128,96},{160,128},{192,160},{224,192},{256... | collective-permute-start | bytes 12296 | tf_op jit(solution)/shard_map/ppermute | solution.py:23
  123.5 10.3 collective-permute-start.13
  133.9 16.6 %collective-permute-start.15 = (f32[26,1,128]{2,1,0:T(1,128)S(1)}, f32[26,1,128]{2,1,0:T(1,128)S(1)}, u32[]{:S(2)}, u32[]{:S(2)}) collective-permute-start(f32[26,1,128]{2,1,0:T(1,128)S(1)} %get-tuple-element.204), channel_id=1, source_target_pairs={{0,1},{1,2},{2,3},{3,4},{4,5},{5,6},{6,7},{7,8},{8,9},{9,10},{10,1... | collective-permute-start | bytes 39944 | tf_op jit(solution)/shard_map/ppermute | solution.py:20
  136.7 13.8 %collective-permute-start.14 = (f32[26,1,128]{2,1,0:T(1,128)S(1)}, f32[26,1,128]{2,1,0:T(1,128)S(1)}, u32[]{:S(2)}, u32[]{:S(2)}) collective-permute-start(f32[26,1,128]{2,1,0:T(1,128)S(1)} %get-tuple-element.203), channel_id=1, source_target_pairs={{1,0},{2,1},{3,2},{4,3},{5,4},{6,5},{7,6},{8,7},{9,8},{10,9},{11,1... | collective-permute-start | bytes 39944 | tf_op jit(solution)/shard_map/ppermute | solution.py:23
  161.6 12.8 %collective-permute-start.16 = (f32[1,4,64]{2,1,0:T(4,128)S(1)}, f32[1,4,64]{2,1,0:T(4,128)S(1)}, u32[]{:S(2)}, u32[]{:S(2)}) collective-permute-start(f32[1,4,64]{2,1,0:T(4,128)S(1)} %get-tuple-element.237), channel_id=1, source_target_pairs={{32,0},{64,32},{96,64},{128,96},{160,128},{192,160},{224,192},{256... | collective-permute-start | bytes 3080 | tf_op jit(solution)/shard_map/ppermute | solution.py:23
  163.6 10.9 %collective-permute-start.17 = (f32[1,4,64]{2,1,0:T(4,128)S(1)}, f32[1,4,64]{2,1,0:T(4,128)S(1)}, u32[]{:S(2)}, u32[]{:S(2)}) collective-permute-start(f32[1,4,64]{2,1,0:T(4,128)S(1)} %get-tuple-element.236), channel_id=1, source_target_pairs={{0,32},{32,64},{64,96},{96,128},{128,160},{160,192},{192,224},{224... | collective-permute-start | bytes 3080 | tf_op jit(solution)/shard_map/ppermute | solution.py:20
  188.0 12.1 %collective-permute-start.20 = (f32[1,4,64]{2,1,0:T(4,128)S(1)}, f32[1,4,64]{2,1,0:T(4,128)S(1)}, u32[]{:S(2)}, u32[]{:S(2)}) collective-permute-start(f32[1,4,64]{2,1,0:T(4,128)S(1)} %get-tuple-element.235), channel_id=1, source_target_pairs={{32,0},{64,32},{96,64},{128,96},{160,128},{192,160},{224,192},{256... | collective-permute-start | bytes 3080 | tf_op jit(solution)/shard_map/ppermute | solution.py:23
  190.0 10.6 %collective-permute-start.21 = (f32[1,4,64]{2,1,0:T(4,128)S(1)}, f32[1,4,64]{2,1,0:T(4,128)S(1)}, u32[]{:S(2)}, u32[]{:S(2)}) collective-permute-start(f32[1,4,64]{2,1,0:T(4,128)S(1)} %get-tuple-element.234), channel_id=1, source_target_pairs={{0,32},{32,64},{64,96},{96,128},{128,160},{160,192},{192,224},{224... | collective-permute-start | bytes 3080 | tf_op jit(solution)/shard_map/ppermute | solution.py:20
  211.6 12.1 %collective-permute-start.24 = (f32[1,2,32]{2,1,0:T(2,128)S(1)}, f32[1,2,32]{2,1,0:T(2,128)S(1)}, u32[]{:S(2)}, u32[]{:S(2)}) collective-permute-start(f32[1,2,32]{2,1,0:T(2,128)S(1)} %get-tuple-element.253), channel_id=1, source_target_pairs={{32,0},{64,32},{96,64},{128,96},{160,128},{192,160},{224,192},{256... | collective-permute-start | bytes 776 | tf_op jit(solution)/shard_map/ppermute | solution.py:23
  213.5 10.6 %collective-permute-start.25 = (f32[1,2,32]{2,1,0:T(2,128)S(1)}, f32[1,2,32]{2,1,0:T(2,128)S(1)}, u32[]{:S(2)}, u32[]{:S(2)}) collective-permute-start(f32[1,2,32]{2,1,0:T(2,128)S(1)} %get-tuple-element.252), channel_id=1, source_target_pairs={{0,32},{32,64},{64,96},{96,128},{128,160},{160,192},{192,224},{224... | collective-permute-start | bytes 776 | tf_op jit(solution)/shard_map/ppermute | solution.py:20
  234.1 12.1 %collective-permute-start.28 = (f32[1,2,32]{2,1,0:T(2,128)S(1)}, f32[1,2,32]{2,1,0:T(2,128)S(1)}, u32[]{:S(2)}, u32[]{:S(2)}) collective-permute-start(f32[1,2,32]{2,1,0:T(2,128)S(1)} %get-tuple-element.251), channel_id=1, source_target_pairs={{32,0},{64,32},{96,64},{128,96},{160,128},{192,160},{224,192},{256... | collective-permute-start | bytes 776 | tf_op jit(solution)/shard_map/ppermute | solution.py:23
  236.1 10.6 %collective-permute-start.29 = (f32[1,2,32]{2,1,0:T(2,128)S(1)}, f32[1,2,32]{2,1,0:T(2,128)S(1)}, u32[]{:S(2)}, u32[]{:S(2)}) collective-permute-start(f32[1,2,32]{2,1,0:T(2,128)S(1)} %get-tuple-element.250), channel_id=1, source_target_pairs={{0,32},{32,64},{64,96},{96,128},{128,160},{160,192},{192,224},{224... | collective-permute-start | bytes 776 | tf_op jit(solution)/shard_map/ppermute | solution.py:20
  256.9 11.9 %collective-permute-start = (f32[1,1,16]{2,1,0:T(1,128)S(1)}, f32[1,1,16]{2,1,0:T(1,128)S(1)}, u32[]{:S(2)}, u32[]{:S(2)}) collective-permute-start(f32[1,1,16]{2,1,0:T(1,128)S(1)} %get-tuple-element.327), channel_id=1, source_target_pairs={{0,32},{32,64},{64,96},{96,128},{128,160},{160,192},{192,224},{224... | collective-permute-start | bytes 200 | tf_op jit(solution)/shard_map/while/body/eval_jaxpr/ppermute | solution.py:20
  266.8 10.3 collective-permute-start.1
  289.6 10.3 collective-permute-start.1
  312.0 10.3 collective-permute-start.1
  334.5 10.3 collective-permute-start.1
  916.5 11.3 %collective-permute-start.32 = (f32[1,2,32]{2,1,0:T(2,128)S(1)}, f32[1,2,32]{2,1,0:T(2,128)S(1)}, u32[]{:S(2)}, u32[]{:S(2)}) collective-permute-start(f32[1,2,32]{2,1,0:T(2,128)S(1)} %get-tuple-element.249), channel_id=1, source_target_pairs={{32,0},{64,32},{96,64},{128,96},{160,128},{192,160},{224,192},{256... | collective-permute-start | bytes 776 | tf_op jit(solution)/shard_map/ppermute | solution.py:23
  939.0 11.9 %collective-permute-start.36 = (f32[1,2,32]{2,1,0:T(2,128)S(1)}, f32[1,2,32]{2,1,0:T(2,128)S(1)}, u32[]{:S(2)}, u32[]{:S(2)}) collective-permute-start(f32[1,2,32]{2,1,0:T(2,128)S(1)} %get-tuple-element.247), channel_id=1, source_target_pairs={{32,0},{64,32},{96,64},{128,96},{160,128},{192,160},{224,192},{256... | collective-permute-start | bytes 776 | tf_op jit(solution)/shard_map/ppermute | solution.py:23
  940.9 10.6 %collective-permute-start.37 = (f32[1,2,32]{2,1,0:T(2,128)S(1)}, f32[1,2,32]{2,1,0:T(2,128)S(1)}, u32[]{:S(2)}, u32[]{:S(2)}) collective-permute-start(f32[1,2,32]{2,1,0:T(2,128)S(1)} %get-tuple-element.246), channel_id=1, source_target_pairs={{0,32},{32,64},{64,96},{96,128},{128,160},{160,192},{192,224},{224... | collective-permute-start | bytes 776 | tf_op jit(solution)/shard_map/ppermute | solution.py:20
  962.1 11.9 %collective-permute-start.40 = (f32[1,4,64]{2,1,0:T(4,128)S(1)}, f32[1,4,64]{2,1,0:T(4,128)S(1)}, u32[]{:S(2)}, u32[]{:S(2)}) collective-permute-start(f32[1,4,64]{2,1,0:T(4,128)S(1)} %get-tuple-element.233), channel_id=1, source_target_pairs={{32,0},{64,32},{96,64},{128,96},{160,128},{192,160},{224,192},{256... | collective-permute-start | bytes 3080 | tf_op jit(solution)/shard_map/ppermute | solution.py:23
  964.1 10.6 %collective-permute-start.41 = (f32[1,4,64]{2,1,0:T(4,128)S(1)}, f32[1,4,64]{2,1,0:T(4,128)S(1)}, u32[]{:S(2)}, u32[]{:S(2)}) collective-permute-start(f32[1,4,64]{2,1,0:T(4,128)S(1)} %get-tuple-element.232), channel_id=1, source_target_pairs={{0,32},{32,64},{64,96},{96,128},{128,160},{160,192},{192,224},{224... | collective-permute-start | bytes 3080 | tf_op jit(solution)/shard_map/ppermute | solution.py:20
  984.7 11.9 %collective-permute-start.44 = (f32[1,4,64]{2,1,0:T(4,128)S(1)}, f32[1,4,64]{2,1,0:T(4,128)S(1)}, u32[]{:S(2)}, u32[]{:S(2)}) collective-permute-start(f32[1,4,64]{2,1,0:T(4,128)S(1)} %get-tuple-element.231), channel_id=1, source_target_pairs={{32,0},{64,32},{96,64},{128,96},{160,128},{192,160},{224,192},{256... | collective-permute-start | bytes 3080 | tf_op jit(solution)/shard_map/ppermute | solution.py:23
  986.6 10.6 %collective-permute-start.45 = (f32[1,4,64]{2,1,0:T(4,128)S(1)}, f32[1,4,64]{2,1,0:T(4,128)S(1)}, u32[]{:S(2)}, u32[]{:S(2)}) collective-permute-start(f32[1,4,64]{2,1,0:T(4,128)S(1)} %get-tuple-element.230), channel_id=1, source_target_pairs={{0,32},{32,64},{64,96},{96,128},{128,160},{160,192},{192,224},{224... | collective-permute-start | bytes 3080 | tf_op jit(solution)/shard_map/ppermute | solution.py:20
  1016.4 11.9 %collective-permute-start.48 = (f32[1,8,128]{2,1,0:T(8,128)S(1)}, f32[1,8,128]{2,1,0:T(8,128)S(1)}, u32[]{:S(2)}, u32[]{:S(2)}) collective-permute-start(f32[1,8,128]{2,1,0:T(8,128)S(1)} %get-tuple-element.212), channel_id=1, source_target_pairs={{32,0},{64,32},{96,64},{128,96},{160,128},{192,160},{224,192},{256... | collective-permute-start | bytes 12296 | tf_op jit(solution)/shard_map/ppermute | solution.py:23
  1018.4 10.7 %collective-permute-start.49 = (f32[1,8,128]{2,1,0:T(8,128)S(1)}, f32[1,8,128]{2,1,0:T(8,128)S(1)}, u32[]{:S(2)}, u32[]{:S(2)}) collective-permute-start(f32[1,8,128]{2,1,0:T(8,128)S(1)} %get-tuple-element.211), channel_id=1, source_target_pairs={{0,32},{32,64},{64,96},{96,128},{128,160},{160,192},{192,224},{224... | collective-permute-start | bytes 12296 | tf_op jit(solution)/shard_map/ppermute | solution.py:20
  1039.2 11.9 %collective-permute-start.52 = (f32[1,8,128]{2,1,0:T(8,128)S(1)}, f32[1,8,128]{2,1,0:T(8,128)S(1)}, u32[]{:S(2)}, u32[]{:S(2)}) collective-permute-start(f32[1,8,128]{2,1,0:T(8,128)S(1)} %get-tuple-element.210), channel_id=1, source_target_pairs={{32,0},{64,32},{96,64},{128,96},{160,128},{192,160},{224,192},{256... | collective-permute-start | bytes 12296 | tf_op jit(solution)/shard_map/ppermute | solution.py:23
  1041.1 10.7 %collective-permute-start.53 = (f32[1,8,128]{2,1,0:T(8,128)S(1)}, f32[1,8,128]{2,1,0:T(8,128)S(1)}, u32[]{:S(2)}, u32[]{:S(2)}) collective-permute-start(f32[1,8,128]{2,1,0:T(8,128)S(1)} %get-tuple-element.209), channel_id=1, source_target_pairs={{0,32},{32,64},{64,96},{96,128},{128,160},{160,192},{192,224},{224... | collective-permute-start | bytes 12296 | tf_op jit(solution)/shard_map/ppermute | solution.py:20
  (136 other events, 920.5 us)
where the time goes:
time: 1070 us; the launch traced here: 1060 us
  starting transfers between devices  529 us (49%)
  waiting for transfers between devices  415 us (39%)
  local copies, waits for them, and re-layouts  81.6 us (8%)
  other arithmetic  33.8 us (3%)
    ppermute x84, waiting for transfers between devices, with_halo(): lax.ppermute(lax.slice_in_dim(block, 0, width, axis=dim), axis, backward)  409 us
    ppermute x84, starting transfers between devices, with_halo(): lax.ppermute(lax.slice_in_dim(block, block.shape[dim] - width, None, axis...  326 us
    ppermute x84, starting transfers between devices, with_halo(): lax.ppermute(lax.slice_in_dim(block, 0, width, axis=dim), axis, backward)  204 us
    reshape x20, local copies, waits for them, and re-layouts, blocks(): return array.reshape(size_a // 2, 2, size_b // 2, 2, size_c // 2, 2)  59.6 us
  transfers between devices with their start and end apart: 168, of which 79 were waited for; matrix products, arithmetic and copies ran while one was open for 8% of the time, Pallas kernels for 0%

commit v1 on v0

v1 whole, which is shorter than its diff:
```python
import jax
import jax.numpy as jnp
from jax import lax
from jax.experimental import pallas as pl
from jax.experimental.pallas import tpu as pltpu
from jax.sharding import PartitionSpec as P

COARSE_ITERS = 30

edge_beta = 3.0
seed_gamma = 4.0
base_mass = 0.1
damping = 0.7

MESH = pl.DeviceIdType.MESH
f32 = jnp.float32

BX, BY, BZ = 24, 8, 128
GX, GY = 16, 32

NEAR = [(dx, dy) for dx in (-1, 0, 1) for dy in (-1, 0, 1) if (dx, dy) != (0, 0)]
WIDE = [(dx, dy) for dx in (-1, 0, 1) for dy in range(-3, 4) if (dx, dy) != (0, 0)]


def place(shape, axis):
    return lax.broadcasted_iota(jnp.int32, shape, axis)


def up(array, distance, axis):
    return pltpu.roll(array, array.shape[axis] - distance, axis)


def down(array, distance, axis):
    return pltpu.roll(array, distance, axis)


def odd(array, distance, axis):
    return (place(array.shape, axis) // distance) % 2 == 1


def high(array, distance, axis):
    return jnp.where(odd(array, distance, axis), array, up(array, distance, axis))


def low(array, distance, axis):
    return jnp.where(odd(array, distance, axis), down(array, distance, axis), array)


def pair(array, distance, axis):
    return array + jnp.where(
        odd(array, distance, axis), down(array, distance, axis), up(array, distance, axis)
    )


def halves(array):
    split = array.reshape((array.shape[0] // 2, 2) + array.shape[1:])
    return split[:, 0], split[:, 1]


def pair_x(array):
    first, second = halves(array)
    return first + second


def coarsen(operator, distance):
    px, py, my, pz, mass = operator
    next_px = jnp.concatenate([px[0:1], halves(px[1:])[1]], axis=0)
    next_px = pair(pair(next_px, distance, 1), distance, 2)
    next_py = high(pair(pair_x(py), distance, 2), distance, 1)
    next_my = low(pair(pair_x(my), distance, 2), distance, 1)
    next_pz = high(pair(pair_x(pz), distance, 1), distance, 2)
    next_mass = pair(pair(pair_x(mass), distance, 1), distance, 2)
    return next_px, next_py, next_my, next_pz, next_mass


def own_diagonal(operator, distance):
    px, py, my, pz, mass = operator
    return mass + px[1:] + px[:-1] + py + my + pz + down(pz, distance, 2)


def weight(upper, lower):
    gap = upper - lower
    return jnp.exp(gap * gap * (-edge_beta / (255.0 * 255.0)))


def step(source, first, count, weights, rhs, dist_y, dist_z, rows=None):
    v = source[pl.ds(first - 1, count + 2)]
    c = v[1:-1]
    near = [v[2:], v[:-2], up(c, dist_y, 1), down(c, dist_y, 1), up(c, dist_z, 2), down(c, dist_z, 2)]
    rows = c.shape[1] if rows is None else rows
    here = c[:, :rows]
    total = (1.0 - damping) * here + rhs[pl.ds(first, count), 0:rows, :]
    for w, n in zip(weights, near):
        total = total + w[pl.ds(first, count), 0:rows, :] * n[:, :rows]
    return here, total


def sweep(source, target, first, last, count, weights, rhs, dist_y, dist_z):
    def turn(index, carry):
        at = first + index * count
        _, total = step(source, at, count, weights, rhs, dist_y, dist_z)
        target[pl.ds(at, count)] = total
        return carry

    lax.fori_loop(0, (last + 1 - first) // count, turn, 0)


def normalise(px, px_before, py, my, pz, mz, mass, stores, at, count):
    diagonal = mass + px + px_before + py + my + pz + mz
    scale = damping / diagonal
    for store, value in zip(stores, (px, px_before, py, my, pz, mz)):
        store[pl.ds(at, count)] = value * scale
    return diagonal, scale


def all_bytes(ref, sem):
    pltpu.make_async_copy(ref, ref, sem).wait()


def kernel(
    ints, labels, out,
    ibuf, lbuf, w0, b0, d0, fine, va0, vb0,
    p1, b1, w1, d1, va1, vb1,
    p2, b2, w2, d2, va2, vb2,
    o3, g1o, q6o, g2o, s3, g1, q6, g2, w3, solved,
    local_sem, send_sem, recv_sem,
):
    gx, gy = lax.axis_index("gx"), lax.axis_index("gy")

    def device(dx, dy):
        return (lax.rem(gx + dx + GX, GX), lax.rem(gy + dy + GY, GY))

    def send(source, target, which, dx, dy):
        pltpu.make_async_remote_copy(
            source, target, send_sem.at[which], recv_sem.at[which],
            device_id=device(dx, dy), device_id_type=MESH,
        ).start()

    own_i = pltpu.make_async_copy(ints, ibuf.at[4:28, 0:8], local_sem.at[0])
    own_l = pltpu.make_async_copy(labels, lbuf.at[4:28, 0:8], local_sem.at[1])
    own_i.start()
    own_l.start()
    p2[:, 8:10, :] = jnp.ones((18, 2, BZ), f32)
    b2[:, 8:10, :] = jnp.zeros((18, 2, BZ), f32)
    barrier = pltpu.get_barrier_semaphore()

    def greet(dx, dy):
        pl.semaphore_signal(barrier, inc=1, device_id=device(dx, dy), device_id_type=MESH)

    def greet_x(dx, carry):
        greet(dx, 0)
        return carry

    def greet_y(dy, carry):
        greet(0, dy)
        return carry

    for dx, dy in WIDE:
        if dx and dy:
            greet(dx, dy)
    lax.fori_loop(1, GX, greet_x, 0)
    lax.fori_loop(1, GY, greet_y, 0)
    pl.semaphore_wait(barrier, 12 + (GX - 1) + (GY - 1))

    for dx, dy in NEAR:
        sx, tx = {1: (pl.ds(20, 4), pl.ds(0, 4)), -1: (pl.ds(0, 4), pl.ds(28, 4)), 0: (pl.ds(0, 24), pl.ds(4, 24))}[dx]
        sy, ty = {1: (pl.ds(4, 4), pl.ds(12, 4)), -1: (pl.ds(0, 4), pl.ds(8, 4)), 0: (pl.ds(0, 8), pl.ds(0, 8))}[dy]
        send(ints.at[sx, sy], ibuf.at[tx, ty], 0, dx, dy)
        send(labels.at[sx, sy], lbuf.at[tx, ty], 1, dx, dy)
    own_i.wait()
    own_l.wait()
    all_bytes(ibuf.at[0:20], recv_sem.at[0])
    all_bytes(lbuf.at[0:20], recv_sem.at[1])

    count = 5

    def fine_turn(index, carry):
        at = 1 + index * count
        wide = ibuf[pl.ds(at - 1, count + 2)].astype(f32)
        lab = lbuf[pl.ds(at, count)]
        c = wide[1:-1]
        px = weight(wide[1:], wide[:-1])
        gone_x = gx * BX + (at - 5) + place(px.shape, 0)
        px = jnp.where((gone_x == GX * BX - 1) | (gone_x == -1), 0.0, px)
        row = place(c.shape, 1)
        gone_y = gy * BY + jnp.where(row >= 12, row - 16, row)
        py = jnp.where((gone_y == GY * BY - 1) | (gone_y == -1), 0.0, weight(up(c, 1, 1), c))
        my = down(py, 1, 1)
        pz = jnp.where(place(c.shape, 2) == BZ - 1, 0.0, weight(up(c, 1, 2), c))
        mz = down(pz, 1, 2)
        mass = base_mass + jnp.where(lab > 0, seed_gamma, 0.0)
        diagonal, scale = normalise(px[1:], px[:-1], py, my, pz, mz, mass, w0, at, count)
        b0[pl.ds(at, count)] = jnp.where(lab == 1, seed_gamma, 0.0) * scale
        d0[pl.ds(at, count)] = diagonal[:, 0:8] * (1.0 / damping)
        for slot, value in enumerate((px[1:], py, my, pz, mass)):
            fine[slot, pl.ds(at, count)] = value[:, 0:8]
        return carry

    lax.fori_loop(0, 30 // count, fine_turn, 0)

    op1 = coarsen(
        (fine[0, 3:28], fine[1, 4:28], fine[2, 4:28], fine[3, 4:28], fine[4, 4:28]), 1
    )
    px, py, _, pz, mass = op1
    ybit, zbit = odd(py, 1, 1), odd(py, 1, 2)
    p1[4:16, 0:8, :] = jnp.where(ybit, jnp.where(zbit, mass, pz), jnp.where(zbit, py, px[1:]))

    def send_1(ref, which):
        for dx, dy in NEAR:
            sx, tx = {1: (pl.ds(12, 4), pl.ds(0, 4)), -1: (pl.ds(4, 4), pl.ds(16, 4)), 0: (pl.ds(4, 12), pl.ds(4, 12))}[dx]
            ty = pl.ds({1: 16, -1: 8, 0: 0}[dy], 8)
            send(ref.at[sx, pl.ds(0, 8)], ref.at[tx, ty], which, dx, dy)

    send_1(p1, 2)

    sweep(b0, va0, 2, 29, 4, w0, b0, 1, 1)

    scale1 = damping / own_diagonal(op1, 2)
    d1[...] = scale1

    def residual_0(index, carry):
        at = 4 + 8 * index
        here, total = step(va0, at, 8, w0, b0, 1, 1, 8)
        r = pair_x(d0[pl.ds(at, 8)] * (total - here))
        r = pair(pair(r, 1, 1), 1, 2)
        b1[pl.ds(4 + 4 * index, 4), 0:8, :] = r * d1[pl.ds(4 * index, 4)]
        return carry

    lax.fori_loop(0, 3, residual_0, 0)
    send_1(b1, 3)

    op2 = coarsen(op1, 2)
    scale2 = damping / own_diagonal(op2, 4)
    d2[...] = scale2
    px, py, _, pz, mass = op2
    slot = place(py.shape, 2) % 4

    def compact(array):
        return jnp.where(place(array.shape, 1) == 0, array, up(array, 3, 1))[:, 0:2]

    p2[6:12, 0:2, :] = compact(
        jnp.where(slot == 0, px[1:], jnp.where(slot == 1, py, jnp.where(slot == 2, pz, mass)))
    )

    def send_2(ref, which):
        for dx, dy in WIDE:
            send(
                ref.at[6:12, 0:2], ref.at[pl.ds(6 * (1 - dx), 6), pl.ds((-2 * dy) % 16, 2)],
                which, dx, dy,
            )

    send_2(p2, 4)

    op3 = coarsen(op2, 4)
    scale3 = damping / own_diagonal(op3, 8)
    px, py, _, pz, mass = op3
    for index, value in enumerate((px[1:], py, pz, mass)):
        o3[3 * index : 3 * index + 3] = value
    g1o[:, pl.ds(gx, 1), :] = o3[:, 0:1, :]

    def gather_x(source, target, which):
        def turn(dx, carry):
            send(source.at[:, 0:1], target.at[:, pl.ds(gx, 1)], which, dx, 0)
            return carry

        lax.fori_loop(1, GX, turn, 0)

    seat = (gy % 4) * 8 + gy // 4

    def gather_y(source, target, which):
        def turn(dy, carry):
            send(source.at[:, 0:1], target.at[:, pl.ds(seat, 1)], which, 0, dy)
            return carry

        target[:, pl.ds(seat, 1), :] = source[:, 0:1, :]
        lax.fori_loop(1, GY, turn, 0)

    def merge_x(source, target, kinds):
        for kind in range(kinds):
            rows = source[3 * kind : 3 * kind + 3]
            mine = place(rows.shape, 2) % 8 == place(rows.shape, 1) // 2
            kept = jnp.where(mine, rows, 0.0)
            kept = kept[:, 0:8] + kept[:, 8:16]
            kept = kept + up(kept, 2, 1)
            kept = kept + up(kept, 4, 1)
            target[6 * kind : 6 * kind + 3] = kept
            target[6 * kind + 3 : 6 * kind + 6] = up(kept, 1, 1)

    gather_x(o3, g1o, 6)

    all_bytes(p1.at[0:16], recv_sem.at[2])

    def weights_1(index, carry):
        at = 1 + 3 * index
        packed = p1[pl.ds(at - 1, 4)]
        even_z, odd_z = low(packed, 1, 2), high(packed[1:], 1, 2)
        px, pz = low(even_z, 1, 1), high(even_z[1:], 1, 1)
        py, mass = low(odd_z, 1, 1), high(odd_z, 1, 1)
        diagonal, _ = normalise(px[1:], px[:-1], py, down(py, 2, 1), pz, down(pz, 2, 2), mass, w1, at, 3)
        va1[pl.ds(at, 3)] = diagonal * (1.0 / damping)
        return carry

    lax.fori_loop(0, 6, weights_1, 0)
    d1[...] = va1[4:16, 0:8, :]
    all_bytes(b1.at[0:16], recv_sem.at[3])
    sweep(b1, va1, 1, 18, 3, w1, b1, 2, 2)

    def residual_1(index, carry):
        at = 4 + 4 * index
        here, total = step(va1, at, 4, w1, b1, 2, 2, 8)
        r = pair_x(d1[pl.ds(4 * index, 4)] * (total - here))
        r = pair(pair(r, 2, 1), 2, 2)
        b2[pl.ds(6 + 2 * index, 2), 0:2, :] = compact(r * d2[pl.ds(2 * index, 2)])
        return carry

    lax.fori_loop(0, 3, residual_1, 0)
    send_2(b2, 5)

    all_bytes(p2.at[0:15], recv_sem.at[4])

    def weights_2(index, carry):
        at = 1 + 4 * index
        packed = p2[pl.ds(at - 1, 5)]
        even_z, odd_z = low(packed, 1, 2), high(packed[1:], 1, 2)
        px, pz = low(even_z, 2, 2), high(even_z[1:], 2, 2)
        py, mass = low(odd_z, 2, 2), high(odd_z, 2, 2)
        diagonal, _ = normalise(px[1:], px[:-1], py, down(py, 1, 1), pz, down(pz, 4, 2), mass, w2, at, 4)
        vb2[pl.ds(at, 4)] = diagonal * (1.0 / damping)
        return carry

    lax.fori_loop(0, 4, weights_2, 0)
    all_bytes(g1o.at[:, 0:15], recv_sem.at[6])
    merge_x(g1o, q6o, 4)
    gather_y(q6o, g2o, 7)

    all_bytes(b2.at[0:15], recv_sem.at[5])
    sweep(b2, va2, 2, 15, 2, w2, b2, 1, 4)
    here, total = step(va2, 6, 6, w2, b2, 1, 4, 8)
    r = pair_x(vb2[6:12, 0:8, :] * (total - here))
    r = pair(pair(r, 1, 1), 4, 2)
    s3[...] = r * scale3
    g1[:, pl.ds(gx, 1), :] = s3[:, 0:1, :]
    gather_x(s3, g1, 8)

    whole = (6, 4, 8, BZ)
    all_bytes(g2o.at[:, 0:31], recv_sem.at[7])
    px, py, pz, mass = [g2o[6 * k : 6 * k + 6].reshape(whole) for k in range(4)]

    def up_x(v):
        return jnp.concatenate([v[1:], up(v[0], 1, 2)[None]], axis=0)

    def down_x(v):
        return jnp.concatenate([down(v[5], 1, 2)[None], v[:5]], axis=0)

    def up_y(v):
        return jnp.concatenate([v[:, 1:], up(v[:, 0], 1, 1)[:, None]], axis=1)

    def down_y(v):
        return jnp.concatenate([down(v[:, 3], 1, 1)[:, None], v[:, :3]], axis=1)

    def lanes(v, shift):
        return pltpu.roll(v.reshape(24, 8, BZ), shift, 2).reshape(whole)

    mx, my, mz = down_x(px), down_y(py), lanes(pz, 8)
    scale = damping / (mass + px + mx + py + my + pz + mz)
    for index, value in enumerate((px, mx, py, my, pz, mz)):
        w3[index] = value * scale

    all_bytes(g1.at[:, 0:15], recv_sem.at[8])
    merge_x(g1, q6, 1)
    gather_y(q6, g2, 9)
    all_bytes(g2.at[:, 0:31], recv_sem.at[9])
    source = g2[...].reshape(whole)

    def solve(index, v):
        near = (up_x(v), down_x(v), up_y(v), down_y(v), lanes(v, BZ - 8), lanes(v, 8))
        total = (1.0 - damping) * v + g2[...].reshape(whole)
        for k, n in enumerate(near):
            total = total + w3[k] * n
        return total

    solved[...] = lax.fori_loop(1, COARSE_ITERS, solve, source).reshape(6, 32, BZ)

    row = (place((16, BZ), 0) // 2 + 2) % 8
    slot = place((16, BZ), 1) % 8
    for j in range(-2, 5):
        at = lax.rem(3 * gx + j + 48, 48)
        tile = jnp.zeros((16, BZ), f32)
        for k in range(-2, 3):
            y = lax.rem(gy + k + GY, GY)
            line = solved[pl.ds(lax.rem(at, 6), 1), pl.ds((y % 4) * 8 + y // 4, 1), :]
            tile = jnp.where(row == k + 2, line.reshape(1, BZ), tile)
        tile = jnp.where(slot == at // 6, tile, 0.0)
        tile = pair(pair(pair(tile, 1, 1), 2, 1), 4, 1)
        va2[6 + 2 * j : 8 + 2 * j] = va2[6 + 2 * j : 8 + 2 * j] + tile[None]
    sweep(va2, vb2, 3, 14, 2, w2, b2, 1, 4)
    sweep(vb2, va2, 4, 13, 2, w2, b2, 1, 4)

    upper = place((1, 8, BZ), 1) >= 4

    def correct_1(index, carry):
        from_plane = 4 + index
        at = 1 + 2 * index - 1
        tiles = []
        for first in (0, 2, 14):
            a = va2[pl.ds(from_plane, 1), first : first + 1, :]
            b = va2[pl.ds(from_plane, 1), first + 1 : first + 2, :]
            tiles.append(jnp.where(upper, b, a))
        whole_row = jnp.concatenate(tiles, axis=1)
        va1[pl.ds(at, 2)] = va1[pl.ds(at, 2)] + whole_row
        return carry

    lax.fori_loop(0, 10, correct_1, 0)
    sweep(va1, vb1, 2, 17, 2, w1, b1, 2, 2)
    sweep(vb1, va1, 3, 16, 2, w1, b1, 2, 2)

    def correct_0(index, carry):
        at = 2 + 2 * index
        coarse = va1[pl.ds(3 + index, 1)]
        whole_row = jnp.concatenate(
            [coarse[:, 0:8], jnp.where(upper, coarse[:, 16:24], coarse[:, 8:16])], axis=1
        )
        va0[pl.ds(at, 2)] = va0[pl.ds(at, 2)] + whole_row
        return carry

    lax.fori_loop(0, 14, correct_0, 0)
    sweep(va0, vb0, 2, 29, 4, w0, b0, 1, 1)

    def finish(index, carry):
        at = 4 + 4 * index
        _, total = step(vb0, at, 4, w0, b0, 1, 1, 8)
        out[pl.ds(4 * index, 4)] = total
        return carry

    lax.fori_loop(0, 6, finish, 0)

    for which, ref in enumerate(
        (ibuf.at[0:20], lbuf.at[0:20], p1.at[0:16], b1.at[0:16], p2.at[0:15], b2.at[0:15],
         g1o.at[:, 0:15], g2o.at[:, 0:31], g1.at[:, 0:15], g2.at[:, 0:31])
    ):
        all_bytes(ref, send_sem.at[which])


def shards(intensities, labels):
    def vmem(*shape, dtype=f32):
        return pltpu.VMEM(shape, dtype)

    fine_shape, one, two = (32, 16, BZ), (20, 24, BZ), (18, 16, BZ)
    return pl.pallas_call(
        kernel,
        out_shape=jax.ShapeDtypeStruct((BX, BY, BZ), f32),
        in_specs=[pl.BlockSpec(memory_space=pl.ANY)] * 2,
        out_specs=pl.BlockSpec(memory_space=pltpu.VMEM),
        scratch_shapes=[
            vmem(*fine_shape, dtype=jnp.int32), vmem(*fine_shape, dtype=jnp.int32),
            [vmem(*fine_shape)] * 6, vmem(*fine_shape), vmem(32, 8, BZ), vmem(5, 32, 8, BZ),
            vmem(*fine_shape), vmem(*fine_shape),
            vmem(*one), vmem(*one), [vmem(*one)] * 6, vmem(12, 8, BZ), vmem(*one), vmem(*one),
            vmem(*two), vmem(*two), [vmem(*two)] * 6, vmem(6, 8, BZ), vmem(*two), vmem(*two),
            vmem(12, 8, BZ), vmem(12, 16, BZ), vmem(24, 8, BZ), vmem(24, 32, BZ),
            vmem(3, 8, BZ), vmem(3, 16, BZ), vmem(6, 8, BZ), vmem(6, 32, BZ),
            vmem(6, 6, 4, 8, BZ), vmem(6, 32, BZ),
            pltpu.SemaphoreType.DMA((2,)),
            pltpu.SemaphoreType.DMA((10,)),
            pltpu.SemaphoreType.DMA((10,)),
        ],
        compiler_params=pltpu.CompilerParams(
            collective_id=0, has_side_effects=True, vmem_limit_bytes=40 * 1024 * 1024
        ),
        name="v_cycle",
    )(intensities, labels)


def solution(mesh):
    return jax.shard_map(
        shards,
        mesh=mesh,
        in_specs=(P("gx", "gy", None), P("gx", "gy", None)),
        out_specs=P("gx", "gy", None),
        check_vma=False,
    )
```

time: 1070 us -> 70 us (0.07)
  the two profiles are of different devices: /device:TPU:63 before, /device:TPU:1 now
where the time goes in v1:
time: 70 us; the launch traced here: 69.8 us
  Pallas kernels  67.4 us (96%)
  local copies, waits for them, and re-layouts  2.43 us (3%)
    pallas_call x1, Pallas kernels, shards(): pl.pallas_call(kernel, out_shape=jax.ShapeDtypeStruct((BX, BY, BZ), f32),...  67.4 us
    unnamed x5, local copies, waits for them, and re-layouts  2.43 us

profile of v1, /device:TPU:1, one launch (start us, length us, event | category | flops | bytes accessed | tf_op | source)
XLA Modules:
  0.0 69.8 jit_solution(6656188780407172274)
XLA Ops:
  0.0 0.0 copy-start
  0.0 0.9 %copy-done = s32[24,8,128]{2,1,0:T(8,128)S(1)} copy-done((s32[24,8,128]{2,1,0:T(8,128)S(1)}, s32[24,8,128]{2,1,0:T(8,128)}, u32[]{:S(2)}) %copy-start) | copy-done | bytes 98328
  0.9 0.0 copy-start.1
  0.9 0.9 %copy-done.1 = s32[24,8,128]{2,1,0:T(8,128)S(1)} copy-done((s32[24,8,128]{2,1,0:T(8,128)S(1)}, s32[24,8,128]{2,1,0:T(8,128)}, u32[]{:S(2)}) %copy-start.1) | copy-done | bytes 98328
  1.8 67.4 %v_cycle.1 = f32[24,8,128]{2,1,0:T(8,128)S(1)} custom-call(s32[24,8,128]{2,1,0:T(8,128)S(1)} %copy-done, s32[24,8,128]{2,1,0:T(8,128)S(1)} %copy-done.1), custom_call_target="tpu_custom_call" | custom-call | tf_op jit(solution)/shard_map/v_cycle/pallas_call | solution.py:449
  69.2 0.6 copy.4
Async XLA Ops:
  0.0 0.9 %copy-start = (s32[24,8,128]{2,1,0:T(8,128)S(1)}, s32[24,8,128]{2,1,0:T(8,128)}, u32[]{:S(2)}) copy-start(s32[24,8,128]{2,1,0:T(8,128)} %ints.1) | copy-start | bytes 294916
  0.9 0.9 %copy-start.1 = (s32[24,8,128]{2,1,0:T(8,128)S(1)}, s32[24,8,128]{2,1,0:T(8,128)}, u32[]{:S(2)}) copy-start(s32[24,8,128]{2,1,0:T(8,128)} %labels.1) | copy-start | bytes 294916

commit v2 on v1

v2 whole, which is shorter than its diff:
```python
import jax
import jax.numpy as jnp
from jax import lax
from jax.experimental import pallas as pl
from jax.experimental.pallas import tpu as pltpu
from jax.sharding import PartitionSpec as P

COARSE_ITERS = 30

edge_beta = 3.0
seed_gamma = 4.0
base_mass = 0.1
damping = 0.7

MESH = pl.DeviceIdType.MESH
f32 = jnp.float32

BX, BY, BZ = 24, 8, 128
GX, GY = 16, 32

NEAR = [(dx, dy) for dx in (-1, 0, 1) for dy in (-1, 0, 1) if (dx, dy) != (0, 0)]
MIDDLE = [(dx, dy) for dx in (-1, 1, 0) for dy in (0, -1, 1, -2, 2) if (dx, dy) != (0, 0)]


def place(shape, axis):
    return lax.broadcasted_iota(jnp.int32, shape, axis)


def up(array, distance, axis):
    return pltpu.roll(array, array.shape[axis] - distance, axis)


def down(array, distance, axis):
    return pltpu.roll(array, distance, axis)


def odd(array, distance, axis):
    return (place(array.shape, axis) // distance) % 2 == 1


def high(array, distance, axis):
    return jnp.where(odd(array, distance, axis), array, up(array, distance, axis))


def low(array, distance, axis):
    return jnp.where(odd(array, distance, axis), down(array, distance, axis), array)


def pair(array, distance, axis):
    return array + jnp.where(
        odd(array, distance, axis), down(array, distance, axis), up(array, distance, axis)
    )


def halves(array):
    split = array.reshape((array.shape[0] // 2, 2) + array.shape[1:])
    return split[:, 0], split[:, 1]


def pair_x(array):
    first, second = halves(array)
    return first + second


def coarsen(operator, distance):
    px, py, my, pz, mass = operator
    next_px = jnp.concatenate([px[0:1], halves(px[1:])[1]], axis=0)
    next_px = pair(pair(next_px, distance, 1), distance, 2)
    next_py = high(pair(pair_x(py), distance, 2), distance, 1)
    next_my = low(pair(pair_x(my), distance, 2), distance, 1)
    next_pz = high(pair(pair_x(pz), distance, 1), distance, 2)
    next_mass = pair(pair(pair_x(mass), distance, 1), distance, 2)
    return next_px, next_py, next_my, next_pz, next_mass


def own_diagonal(operator, distance):
    px, py, my, pz, mass = operator
    return mass + px[1:] + px[:-1] + py + my + pz + down(pz, distance, 2)


def weight(upper, lower):
    gap = upper - lower
    return jnp.exp(gap * gap * (-edge_beta / (255.0 * 255.0)))


def step(source, first, count, weights, rhs, dist_y, dist_z, rows=None):
    v = source[pl.ds(first - 1, count + 2)]
    c = v[1:-1]
    near = [v[2:], v[:-2], up(c, dist_y, 1), down(c, dist_y, 1), up(c, dist_z, 2), down(c, dist_z, 2)]
    rows = c.shape[1] if rows is None else rows
    here = c[:, :rows]
    total = (1.0 - damping) * here + rhs[pl.ds(first, count), 0:rows, :]
    for w, n in zip(weights, near):
        total = total + w[pl.ds(first, count), 0:rows, :] * n[:, :rows]
    return here, total


def sweep(source, target, first, last, count, weights, rhs, dist_y, dist_z):
    def turn(index, carry):
        at = first + index * count
        _, total = step(source, at, count, weights, rhs, dist_y, dist_z)
        target[pl.ds(at, count)] = total
        return carry

    lax.fori_loop(0, (last + 1 - first) // count, turn, 0, unroll=True)


def normalise(px, px_before, py, my, pz, mz, mass, stores, at, count):
    diagonal = mass + px + px_before + py + my + pz + mz
    scale = damping / diagonal
    for store, value in zip(stores, (px, px_before, py, my, pz, mz)):
        store[pl.ds(at, count)] = value * scale
    return diagonal, scale


def kernel(
    ints, labels, out,
    ibuf, lbuf, w0, b0, d0, fine, va0, vb0,
    p1, b1p, b1, w1, d1, s1, va1, vb1,
    p2, x2, b2, w2, d2, s2, va2, vb2,
    o3, g1o, qo, g2o, o4, g1, q, g2, w3, b3, solved,
    local_sem, send_sem, recv_sem,
):
    gx, gy = lax.axis_index("gx"), lax.axis_index("gy")
    half, chip_y = gx // 8, gx % 8
    chip_z, chip_x, core = half * 4 + gy // 8, gy % 8 // 2, gy % 2
    groups = {}

    def device(dx, dy):
        return (lax.rem(gx + dx + GX, GX), lax.rem(gy + dy + GY, GY))

    def in_plane(k):
        return (half * 8 + (chip_y + k // 2) % 8, gy - core + (core + k) % 2)

    def in_column(k):
        z = (chip_z + k // 4) % 8
        return (z // 4 * 8 + chip_y, z % 4 * 8 + (chip_x + k) % 4 * 2 + core)

    def send(source, target, which, to):
        pltpu.make_async_remote_copy(
            source, target, send_sem.at[which], recv_sem.at[which],
            device_id=to, device_id_type=MESH,
        ).start()

    def each(count, action):
        def turn(index, carry):
            action(index)
            return carry

        lax.fori_loop(1, count, turn, 0)

    def await_bytes(ref, sem):
        pltpu.make_async_copy(ref, ref, sem).wait()

    def arrived(which):
        await_bytes(groups[which], recv_sem.at[which])

    own = [
        pltpu.make_async_copy(ints, ibuf.at[4:28, 0:8], local_sem.at[0]),
        pltpu.make_async_copy(labels, lbuf.at[4:28, 0:8], local_sem.at[1]),
    ]
    for copy in own:
        copy.start()
    barrier = pltpu.get_barrier_semaphore()

    def greet(to):
        pl.semaphore_signal(barrier, inc=1, device_id=to, device_id_type=MESH)

    for dx, dy in MIDDLE:
        greet(device(dx, dy))
    each(16, lambda k: greet(in_plane(k)))
    each(32, lambda k: greet(in_column(k)))
    p2[:, 6:12, :] = jnp.ones((18, 6, BZ), f32)
    x2[:, 6:12, :] = jnp.zeros((18, 6, BZ), f32)
    pl.semaphore_wait(barrier, len(MIDDLE) + 15 + 31)

    def send_inputs(source, target, which, depth, corner_x, corner_y):
        for dx, dy in sorted(NEAR, key=lambda d: (d[0] == 0, d[1] != 0)):
            n, m = (corner_x, corner_y) if dx and dy else (depth, depth)
            sx, tx = {1: (24 - n, 4 - n), -1: (0, 28), 0: (0, 4)}[dx]
            sy, ty = {1: (8 - m, 16 - m), -1: (0, 8), 0: (0, 0)}[dy]
            nx, ny = n if dx else 24, m if dy else 8
            send(
                source.at[sx : sx + nx, sy : sy + ny], target.at[tx : tx + nx, ty : ty + ny],
                which, device(dx, dy),
            )

    send_inputs(ints, ibuf, 0, 4, 3, 4)
    send_inputs(labels, lbuf, 1, 3, 2, 2)
    groups[0] = ibuf.at[0:19]
    groups[1] = lbuf.at[0:13]
    for copy in own:
        copy.wait()
    arrived(0)
    arrived(1)

    count = 5

    def fine_turn(index, carry):
        at = 1 + index * count
        wide = ibuf[pl.ds(at - 1, count + 2)].astype(f32)
        lab = lbuf[pl.ds(at, count)]
        c = wide[1:-1]
        px = weight(wide[1:], wide[:-1])
        gone_x = gx * BX + (at - 5) + place(px.shape, 0)
        px = jnp.where((gone_x == GX * BX - 1) | (gone_x == -1), 0.0, px)
        row = place(c.shape, 1)
        gone_y = gy * BY + jnp.where(row >= 12, row - 16, row)
        py = jnp.where((gone_y == GY * BY - 1) | (gone_y == -1), 0.0, weight(up(c, 1, 1), c))
        my = down(py, 1, 1)
        pz = jnp.where(place(c.shape, 2) == BZ - 1, 0.0, weight(up(c, 1, 2), c))
        mz = down(pz, 1, 2)
        mass = base_mass + jnp.where(lab > 0, seed_gamma, 0.0)
        diagonal, scale = normalise(px[1:], px[:-1], py, my, pz, mz, mass, w0, at, count)
        b0[pl.ds(at, count)] = jnp.where(lab == 1, seed_gamma, 0.0) * scale
        d0[pl.ds(at, count)] = diagonal[:, 0:8] * (1.0 / damping)
        for slot, value in enumerate((px[1:], py, my, pz, mass)):
            fine[slot, pl.ds(at, count)] = value[:, 0:8]
        return carry

    lax.fori_loop(0, 30 // count, fine_turn, 0, unroll=True)

    op1 = coarsen(
        (fine[0, 3:28], fine[1, 4:28], fine[2, 4:28], fine[3, 4:28], fine[4, 4:28]), 1
    )
    px, py, _, pz, mass = op1
    ybit, zbit = odd(py, 1, 1), odd(py, 1, 2)
    p1[6:18, 0:8, :] = jnp.where(ybit, jnp.where(zbit, mass, pz), jnp.where(zbit, py, px[1:]))
    scale1 = damping / own_diagonal(op1, 2)
    s1[...] = scale1

    def send_1(ref, which, near, whole, corners):
        for dx, dy in MIDDLE:
            if abs(dy) == 2:
                parts = [(*{1: (4, 20), -1: (0, 16)}[dy // 2], 4, corners[2])]
            elif dx and dy:
                close, far = {1: ((4, 28), (0, 24)), -1: ((0, 8), (4, 12))}[dy]
                parts = [(*close, 4, corners[0]), (*far, 4, corners[1])]
            else:
                parts = [(0, {0: 0, 1: 24, -1: 8}[dy], 8, near)]
            for sy, ty, ny, n in parts:
                nx = n if dx else whole
                sx = near + (whole - n if dx == 1 else 0)
                tx = {1: near - n, -1: near + whole, 0: near}[dx]
                send(
                    ref.at[sx : sx + nx, sy : sy + ny], ref.at[tx : tx + nx, ty : ty + ny],
                    which, device(dx, dy),
                )

    send_1(p1, 2, 6, 12, (5, 3, 1))
    groups[2] = p1.at[0:24, 0:22]

    sweep(b0, va0, 2, 29, 4, w0, b0, 1, 1)

    def residual_0(index, carry):
        at = 4 + 6 * index
        here, total = step(va0, at, 6, w0, b0, 1, 1, 8)
        r = pair_x(d0[pl.ds(at, 6)] * (total - here))
        r = pair(pair(r, 1, 1), 1, 2) * s1[pl.ds(3 * index, 3)]
        ybit, zbit = odd(r[0:1], 1, 1), odd(r[0:1], 1, 2)
        b1p[pl.ds(2 + index, 1), 0:8, :] = jnp.where(zbit, jnp.where(ybit, r[2:3], r[1:2]), r[0:1])
        return carry

    lax.fori_loop(0, 4, residual_0, 0, unroll=True)
    send_1(b1p, 3, 2, 4, (2, 1, 1))
    groups[3] = b1p.at[0:6]

    op2 = coarsen(op1, 2)
    px, py, _, pz, mass = op2
    slot = place(py.shape, 2) % 4
    packed = jnp.where(slot == 0, px[1:], jnp.where(slot == 1, py, jnp.where(slot == 2, pz, mass)))
    p2[6:12, 0:2, :] = jnp.where(place(packed.shape, 1) == 0, packed, up(packed, 3, 1))[:, 0:2]

    def send_2(ref, which):
        for dx, dy in MIDDLE:
            n = 6 if dx == 0 else 2 if abs(dy) == 2 else 4
            sx = 12 - n if dx == 1 else 6
            tx = {1: 6 - n, -1: 12, 0: 6}[dx]
            ty = -2 * dy % 16
            send(ref.at[sx : sx + n, 0:2], ref.at[tx : tx + n, ty : ty + 2], which, device(dx, dy))
        groups[which] = ref.at[0:7]

    send_2(p2, 4)

    op3 = coarsen(op2, 4)
    s3 = damping / own_diagonal(op3, 8)
    px, py, _, pz, mass = op3
    for index, value in enumerate((px[1:], py, pz, mass)):
        o3[3 * index : 3 * index + 3] = value

    def gather_plane(source, target, which):
        seat = core * 8 + chip_y
        target[:, pl.ds(seat, 1), :] = source[:, 0:1, :]
        each(16, lambda k: send(source.at[:, 0:1], target.at[:, pl.ds(seat, 1)], which, in_plane(k)))
        groups[which] = target.at[:, 0:15]

    def merge(source, target, kinds):
        rows = source[...]
        rows = jnp.where(place(rows.shape, 2) % 8 == place(rows.shape, 1) % 8, rows, 0.0)
        rows = rows.reshape(3 * kinds * 2, 8, BZ)
        for distance in (1, 2, 4):
            rows = rows + up(rows, distance, 1)
        target[...] = rows.reshape(kinds, 3, 2, 8, BZ)

    def gather_column(source, target, which, kinds):
        piece = source.at[kinds, :, :, 0:1]
        seat = target.at[kinds, half, :, pl.ds(gy % 4 // 2 * 2, 2), pl.ds(gy // 4, 1)]
        pltpu.make_async_copy(piece, seat, recv_sem.at[which]).start()
        each(32, lambda k: send(piece, seat, which, in_column(k)))

    gather_plane(o3, g1o, 6)

    arrived(2)

    def weights_1(index, carry):
        at = 1 + 2 * index
        packed = p1[pl.ds(at - 1, 3)]
        even_z, odd_z = low(packed, 1, 2), high(packed[1:], 1, 2)
        px, pz = low(even_z, 1, 1), high(even_z[1:], 1, 1)
        py, mass = low(odd_z, 1, 1), high(odd_z, 1, 1)
        diagonal, _ = normalise(px[1:], px[:-1], py, down(py, 2, 1), pz, down(pz, 2, 2), mass, w1, at, 2)
        d1[pl.ds(at, 2)] = diagonal * (1.0 / damping)
        return carry

    lax.fori_loop(0, 11, weights_1, 0, unroll=True)
    arrived(3)

    def unpack_1(index, carry):
        packed = b1p[pl.ds(index, 1)]
        odd_z = high(packed, 1, 2)
        b1[pl.ds(3 * index, 1)] = low(packed, 1, 2)
        b1[pl.ds(3 * index + 1, 1)] = low(odd_z, 1, 1)
        b1[pl.ds(3 * index + 2, 1)] = high(odd_z, 1, 1)
        return carry

    lax.fori_loop(0, 8, unpack_1, 0, unroll=True)
    sweep(b1, va1, 1, 22, 2, w1, b1, 2, 2)

    arrived(4)

    def weights_2(index, carry):
        at = 1 + 4 * index
        packed = p2[pl.ds(at - 1, 5)]
        even_z, odd_z = low(packed, 1, 2), high(packed[1:], 1, 2)
        px, pz = low(even_z, 2, 2), high(even_z[1:], 2, 2)
        py, mass = low(odd_z, 2, 2), high(odd_z, 2, 2)
        diagonal, scale = normalise(px[1:], px[:-1], py, down(py, 1, 1), pz, down(pz, 4, 2), mass, w2, at, 4)
        d2[pl.ds(at, 4)] = diagonal * (1.0 / damping)
        s2[pl.ds(at, 4)] = scale
        return carry

    lax.fori_loop(0, 4, weights_2, 0, unroll=True)

    def residual_1(index, carry):
        at = 2 + 4 * index
        here, total = step(va1, at, 4, w1, b1, 2, 2)
        r = pair_x(d1[pl.ds(at, 4)] * (total - here))
        r = pair(pair(r, 2, 1), 2, 2)
        mine, after, before = r[:, 0:8], r[:, 8:16], r[:, 24:32]
        row = place(mine.shape, 1)
        first = jnp.where(row < 2, jnp.where(row == 0, mine, up(mine, 3, 1)), jnp.where(row == 2, down(after, 2, 1), up(after, 1, 1)))
        last = jnp.where(row == 7, down(before, 3, 1), up(before, 2, 1))
        to = pl.ds(4 + 2 * index, 2)
        b2[to, 0:8, :] = first * s2[to, 0:8, :]
        b2[to, 8:16, :] = last * s2[to, 8:16, :]
        return carry

    lax.fori_loop(0, 5, residual_1, 0, unroll=True)

    sweep(b2, va2, 5, 12, 4, w2, b2, 1, 4)
    here, total = step(va2, 6, 6, w2, b2, 1, 4, 8)
    r = pair_x(d2[6:12, 0:8, :] * (total - here))
    r = pair(pair(r, 1, 1), 4, 2)
    o4[...] = r * s3
    gather_plane(o4, g1, 8)

    arrived(6)
    merge(g1o, qo, 4)
    half_kinds = pl.ds(2 * core, 2)
    gather_column(qo, g2o, 7, half_kinds)
    groups[7] = g2o.at[0:2]
    zbit = odd(here[:, 0:2], 1, 2)
    x2[6:12, 0:2, :] = jnp.where(zbit, b2[6:12, 0:2, :], here[:, 0:2])
    send_2(x2, 5)

    arrived(8)
    merge(g1, q, 1)
    gather_column(q, g2, 9, pl.ds(0, 1))
    groups[9] = g2

    arrived(7)
    send(g2o.at[half_kinds], g2o.at[half_kinds], 10, (gx, gy + 1 - 2 * core))
    groups[10] = g2o.at[0:2]
    arrived(5)
    b2[...] = high(x2[...], 1, 2)
    va2[...] = low(x2[...], 1, 2)

    whole = (3, 4, 2, 8, BZ)

    def lanes(v, shift):
        return pltpu.roll(v.reshape(-1, 8, BZ), shift, 2).reshape(v.shape)

    def rows(v, shift):
        return pltpu.roll(v.reshape(-1, 8, BZ), shift, 1).reshape(v.shape)

    def spread(v):
        second = odd(v[0], 8, 3)
        return jnp.stack(
            [jnp.where(second, lanes(v[1], 8), v[0]), jnp.where(second, v[1], lanes(v[0], BZ - 8))],
            axis=2,
        )

    def around(v):
        return (
            jnp.concatenate([v[1:], lanes(v[:1], BZ - 1)], axis=0),
            jnp.concatenate([lanes(v[2:], 1), v[:2]], axis=0),
            jnp.concatenate([v[:, 1:], rows(v[:, :1], 7)], axis=1),
            jnp.concatenate([rows(v[:, 3:], 1), v[:, :3]], axis=1),
            jnp.concatenate([v[:, :, 1:], lanes(v[:, :, :1], BZ - 16)], axis=2),
            jnp.concatenate([lanes(v[:, :, 1:], 16), v[:, :, :1]], axis=2),
        )

    arrived(10)
    px, py, pz, mass = [spread(g2o[k]) for k in range(4)]
    mx, my, mz = around(px)[1], around(py)[3], around(pz)[5]
    scale = damping / (mass + px + mx + py + my + pz + mz)
    for index, value in enumerate((px, mx, py, my, pz, mz)):
        w3[index] = value * scale
    arrived(9)
    b3[...] = spread(g2[0])

    def solve(index, v):
        total = (1.0 - damping) * v + b3[...]
        for k, n in enumerate(around(v)):
            total = total + w3[k] * n
        return total

    solved[...] = lax.fori_loop(1, COARSE_ITERS, solve, b3[...], unroll=True)

    row = (place((16, BZ), 0) // 2 + 2) % 8
    slot = place((16, BZ), 1) % 16
    for j in range(-2, 5):
        at = (3 * gx + j + 48) % 48
        tiles = []
        for z_low in range(2):
            tile = jnp.zeros((16, BZ), f32)
            for k in range(-2, 3):
                y = (gy + k + GY) % GY
                line = solved[pl.ds(at % 3, 1), pl.ds(y % 4, 1), z_low, pl.ds(y // 4, 1), :]
                tile = jnp.where(row == k + 2, line.reshape(1, BZ), tile)
            tiles.append(pair(jnp.where(slot == at // 3, tile, 0.0), 8, 1))
        tile = jnp.where(slot >= 8, tiles[1], tiles[0])
        tile = pair(pair(pair(tile, 1, 1), 2, 1), 4, 1)
        va2[6 + 2 * j : 8 + 2 * j] = va2[6 + 2 * j : 8 + 2 * j] + tile[None]
    sweep(va2, vb2, 3, 14, 4, w2, b2, 1, 4)
    sweep(vb2, va2, 4, 13, 5, w2, b2, 1, 4)

    upper = place((1, 8, BZ), 1) >= 4

    def correct_1(index, carry):
        for rows, first in ((0, 0), (8, 2), (24, 14)):
            a = va2[pl.ds(4 + index, 1), first : first + 1, :]
            b = va2[pl.ds(4 + index, 1), first + 1 : first + 2, :]
            at = pl.ds(2 + 2 * index, 2)
            va1[at, rows : rows + 8, :] = va1[at, rows : rows + 8, :] + jnp.where(upper, b, a)
        return carry

    lax.fori_loop(0, 10, correct_1, 0, unroll=True)
    sweep(va1, vb1, 4, 19, 2, w1, b1, 2, 2)
    sweep(vb1, va1, 5, 18, 2, w1, b1, 2, 2)

    def correct_0(index, carry):
        at = pl.ds(2 + 2 * index, 2)
        coarse = va1[pl.ds(5 + index, 1)]
        va0[at, 0:8, :] = va0[at, 0:8, :] + coarse[:, 0:8]
        va0[at, 8:16, :] = va0[at, 8:16, :] + jnp.where(upper, coarse[:, 24:32], coarse[:, 8:16])
        return carry

    lax.fori_loop(0, 14, correct_0, 0, unroll=True)
    sweep(va0, vb0, 2, 29, 4, w0, b0, 1, 1)

    def finish(index, carry):
        at = 4 + 4 * index
        _, total = step(vb0, at, 4, w0, b0, 1, 1, 8)
        out[pl.ds(4 * index, 4)] = total
        return carry

    lax.fori_loop(0, 6, finish, 0, unroll=True)

    for which in (0, 1, 2, 3, 4, 5, 6, 8, 10):
        await_bytes(groups[which], send_sem.at[which])
    await_bytes(p1.at[0:12, 0:31], send_sem.at[7])
    await_bytes(p1.at[0:6, 0:31], send_sem.at[9])


def shards(intensities, labels):
    def vmem(*shape, dtype=f32):
        return pltpu.VMEM(shape, dtype)

    zero, one, two = (32, 16, BZ), (24, 32, BZ), (18, 16, BZ)
    return pl.pallas_call(
        kernel,
        out_shape=jax.ShapeDtypeStruct((BX, BY, BZ), f32),
        in_specs=[pl.BlockSpec(memory_space=pltpu.HBM)] * 2,
        out_specs=pl.BlockSpec(memory_space=pltpu.VMEM),
        scratch_shapes=[
            vmem(*zero, dtype=jnp.int32), vmem(*zero, dtype=jnp.int32),
            [vmem(*zero)] * 6, vmem(*zero), vmem(32, 8, BZ), vmem(5, 32, 8, BZ),
            vmem(*zero), vmem(*zero),
            vmem(*one), vmem(8, 32, BZ), vmem(*one), [vmem(*one)] * 6, vmem(*one), vmem(12, 8, BZ),
            vmem(*one), vmem(*one),
            vmem(*two), vmem(*two), vmem(*two), [vmem(*two)] * 6, vmem(*two), vmem(*two),
            vmem(*two), vmem(*two),
            vmem(12, 8, BZ), vmem(12, 16, BZ), vmem(4, 3, 2, 8, BZ), vmem(4, 2, 3, 4, 8, BZ),
            vmem(3, 8, BZ), vmem(3, 16, BZ), vmem(1, 3, 2, 8, BZ), vmem(1, 2, 3, 4, 8, BZ),
            vmem(6, 3, 4, 2, 8, BZ), vmem(3, 4, 2, 8, BZ), vmem(3, 4, 2, 8, BZ),
            pltpu.SemaphoreType.DMA((2,)),
            pltpu.SemaphoreType.DMA((11,)),
            pltpu.SemaphoreType.DMA((11,)),
        ],
        compiler_params=pltpu.CompilerParams(
            collective_id=0, has_side_effects=True, vmem_limit_bytes=40 * 1024 * 1024
        ),
        name="v_cycle",
    )(intensities, labels)


def solution(mesh):
    return jax.shard_map(
        shards,
        mesh=mesh,
        in_specs=(P("gx", "gy", None), P("gx", "gy", None)),
        out_specs=P("gx", "gy", None),
        check_vma=False,
    )
```

time: 70 us -> 52.9 us (0.76)
  Pallas kernels: 67.4 us -> 50.1 us
    pallas_call x1, Pallas kernels: 67.4 us -> 50.1 us  [shards(): pl.pallas_call(kernel, out_shape=jax.ShapeDtypeStruct((BX, BY, BZ), f32),...]
where the time goes in v2:
time: 52.9 us; the launch traced here: 52.5 us
  Pallas kernels  50.1 us (95%)
  local copies, waits for them, and re-layouts  2.43 us (5%)
    pallas_call x1, Pallas kernels, shards(): pl.pallas_call(kernel, out_shape=jax.ShapeDtypeStruct((BX, BY, BZ), f32),...  50.1 us
    unnamed x5, local copies, waits for them, and re-layouts  2.43 us

profile of v2, /device:TPU:1, one launch (start us, length us, event | category | flops | bytes accessed | tf_op | source)
XLA Modules:
  0.0 52.5 jit_solution(4611521904346584173)
XLA Ops:
  0.0 0.0 copy-start
  0.0 0.9 %copy-done = s32[24,8,128]{2,1,0:T(8,128)S(1)} copy-done((s32[24,8,128]{2,1,0:T(8,128)S(1)}, s32[24,8,128]{2,1,0:T(8,128)}, u32[]{:S(2)}) %copy-start) | copy-done | bytes 98328
  0.9 0.0 copy-start.1
  0.9 0.9 %copy-done.1 = s32[24,8,128]{2,1,0:T(8,128)S(1)} copy-done((s32[24,8,128]{2,1,0:T(8,128)S(1)}, s32[24,8,128]{2,1,0:T(8,128)}, u32[]{:S(2)}) %copy-start.1) | copy-done | bytes 98328
  1.8 50.1 %v_cycle.1 = f32[24,8,128]{2,1,0:T(8,128)S(1)} custom-call(s32[24,8,128]{2,1,0:T(8,128)S(1)} %copy-done, s32[24,8,128]{2,1,0:T(8,128)S(1)} %copy-done.1), custom_call_target="tpu_custom_call" | custom-call | tf_op jit(solution)/shard_map/v_cycle/pallas_call | solution.py:501
  51.9 0.6 %copy.4 = f32[24,8,128]{2,1,0:T(8,128)} copy(f32[24,8,128]{2,1,0:T(8,128)S(1)} %v_cycle.1) | data formatting | bytes 196608
Async XLA Ops:
  0.0 0.9 %copy-start = (s32[24,8,128]{2,1,0:T(8,128)S(1)}, s32[24,8,128]{2,1,0:T(8,128)}, u32[]{:S(2)}) copy-start(s32[24,8,128]{2,1,0:T(8,128)} %ints.1) | copy-start | bytes 294916
  0.9 0.9 %copy-start.1 = (s32[24,8,128]{2,1,0:T(8,128)S(1)}, s32[24,8,128]{2,1,0:T(8,128)}, u32[]{:S(2)}) copy-start(s32[24,8,128]{2,1,0:T(8,128)} %labels.1) | copy-start | bytes 294916

commit v3 on v2

--- a/solution.py
+++ b/solution.py
@@ -115,7 +115,7 @@
 
 def kernel(
     ints, labels, out,
-    ibuf, lbuf, w0, b0, d0, fine, va0, vb0,
+    ibuf, lbuf, obuf, w0, b0, d0, fine, va0, vb0,
     p1, b1p, b1, w1, d1, s1, va1, vb1,
     p2, x2, b2, w2, d2, s2, va2, vb2,
     o3, g1o, qo, g2o, o4, g1, q, g2, w3, b3, solved,
@@ -129,12 +129,16 @@
     def device(dx, dy):
         return (lax.rem(gx + dx + GX, GX), lax.rem(gy + dy + GY, GY))
 
+    def offset(k, size):
+        return (size // 2 + (k + 1) // 2 * (1 - 2 * (k % 2))) % size
+
     def in_plane(k):
-        return (half * 8 + (chip_y + k // 2) % 8, gy - core + (core + k) % 2)
+        return (half * 8 + (chip_y + offset(k // 2, 8)) % 8, gy - core + (core + k + 1) % 2)
 
     def in_column(k):
-        z = (chip_z + k // 4) % 8
-        return (z // 4 * 8 + chip_y, z % 4 * 8 + (chip_x + k) % 4 * 2 + core)
+        z = (chip_z + offset(k // 4, 8)) % 8
+        x = (chip_x + offset(k % 4, 4)) % 4
+        return (z // 4 * 8 + chip_y, z % 4 * 8 + x * 2 + core)
 
     def send(source, target, which, to):
         pltpu.make_async_remote_copy(
@@ -147,7 +151,7 @@
             action(index)
             return carry
 
-        lax.fori_loop(1, count, turn, 0)
+        lax.fori_loop(0, count, turn, 0)
 
     def await_bytes(ref, sem):
         pltpu.make_async_copy(ref, ref, sem).wait()
@@ -168,36 +172,38 @@
 
     for dx, dy in MIDDLE:
         greet(device(dx, dy))
-    each(16, lambda k: greet(in_plane(k)))
-    each(32, lambda k: greet(in_column(k)))
+    each(31, lambda k: greet(in_column(k)))
+    each(15, lambda k: greet(in_plane(k)))
     p2[:, 6:12, :] = jnp.ones((18, 6, BZ), f32)
     x2[:, 6:12, :] = jnp.zeros((18, 6, BZ), f32)
     pl.semaphore_wait(barrier, len(MIDDLE) + 15 + 31)
 
-    def send_inputs(source, target, which, depth, corner_x, corner_y):
-        for dx, dy in sorted(NEAR, key=lambda d: (d[0] == 0, d[1] != 0)):
+    for copy in own:
+        copy.wait()
+
+    def send_inputs(target, which, pairs, depth, corner_x, corner_y):
+        for dx, dy in pairs:
             n, m = (corner_x, corner_y) if dx and dy else (depth, depth)
-            sx, tx = {1: (24 - n, 4 - n), -1: (0, 28), 0: (0, 4)}[dx]
+            sx, tx = {1: (28 - n, 4 - n), -1: (4, 28), 0: (4, 4)}[dx]
             sy, ty = {1: (8 - m, 16 - m), -1: (0, 8), 0: (0, 0)}[dy]
             nx, ny = n if dx else 24, m if dy else 8
             send(
-                source.at[sx : sx + nx, sy : sy + ny], target.at[tx : tx + nx, ty : ty + ny],
+                target.at[sx : sx + nx, sy : sy + ny], target.at[tx : tx + nx, ty : ty + ny],
                 which, device(dx, dy),
             )
 
-    send_inputs(ints, ibuf, 0, 4, 3, 4)
-    send_inputs(labels, lbuf, 1, 3, 2, 2)
-    groups[0] = ibuf.at[0:19]
-    groups[1] = lbuf.at[0:13]
-    for copy in own:
-        copy.wait()
+    aside = [d for d in NEAR if d[0] == 0]
+    ahead = [(1, 0), (-1, 0), (1, 1), (1, -1), (-1, 1), (-1, -1)]
+    send_inputs(ibuf, 11, ahead, 4, 3, 4)
+    send_inputs(lbuf, 12, ahead, 3, 2, 2)
+    send_inputs(ibuf, 0, aside, 4, 3, 4)
+    send_inputs(lbuf, 1, aside, 3, 2, 2)
+    groups[0], groups[1] = ibuf.at[0:12], lbuf.at[0:9]
+    groups[11], groups[12] = ibuf.at[0:7], lbuf.at[0:4]
     arrived(0)
     arrived(1)
 
-    count = 5
-
-    def fine_turn(index, carry):
-        at = 1 + index * count
+    def fine_operator(at, count):
         wide = ibuf[pl.ds(at - 1, count + 2)].astype(f32)
         lab = lbuf[pl.ds(at, count)]
         c = wide[1:-1]
@@ -216,41 +222,60 @@
         d0[pl.ds(at, count)] = diagonal[:, 0:8] * (1.0 / damping)
         for slot, value in enumerate((px[1:], py, my, pz, mass)):
             fine[slot, pl.ds(at, count)] = value[:, 0:8]
-        return carry
-
-    lax.fori_loop(0, 30 // count, fine_turn, 0, unroll=True)
-
-    op1 = coarsen(
-        (fine[0, 3:28], fine[1, 4:28], fine[2, 4:28], fine[3, 4:28], fine[4, 4:28]), 1
-    )
-    px, py, _, pz, mass = op1
-    ybit, zbit = odd(py, 1, 1), odd(py, 1, 2)
-    p1[6:18, 0:8, :] = jnp.where(ybit, jnp.where(zbit, mass, pz), jnp.where(zbit, py, px[1:]))
-    scale1 = damping / own_diagonal(op1, 2)
-    s1[...] = scale1
-
-    def send_1(ref, which, near, whole, corners):
+
+    def level_1(first, last):
+        at, end = 4 + 2 * first, 6 + 2 * last
+        return coarsen((fine[0, at - 1 : end], *(fine[slot, at:end] for slot in range(1, 5))), 1)
+
+    def packed_1(operator):
+        px, py, _, pz, mass = operator
+        ybit, zbit = odd(py, 1, 1), odd(py, 1, 2)
+        return jnp.where(ybit, jnp.where(zbit, mass, pz), jnp.where(zbit, py, px[1:]))
+
+    def send_1(ref, which, near, whole, corners, ends):
         for dx, dy in MIDDLE:
             if abs(dy) == 2:
                 parts = [(*{1: (4, 20), -1: (0, 16)}[dy // 2], 4, corners[2])]
+            elif dx and dy and corners[0] == corners[1]:
+                parts = [(0, {1: 24, -1: 8}[dy], 8, corners[0])]
             elif dx and dy:
                 close, far = {1: ((4, 28), (0, 24)), -1: ((0, 8), (4, 12))}[dy]
                 parts = [(*close, 4, corners[0]), (*far, 4, corners[1])]
             else:
                 parts = [(0, {0: 0, 1: 24, -1: 8}[dy], 8, near)]
             for sy, ty, ny, n in parts:
-                nx = n if dx else whole
-                sx = near + (whole - n if dx == 1 else 0)
-                tx = {1: near - n, -1: near + whole, 0: near}[dx]
-                send(
-                    ref.at[sx : sx + nx, sy : sy + ny], ref.at[tx : tx + nx, ty : ty + ny],
-                    which, device(dx, dy),
-                )
-
-    send_1(p1, 2, 6, 12, (5, 3, 1))
-    groups[2] = p1.at[0:24, 0:22]
-
-    sweep(b0, va0, 2, 29, 4, w0, b0, 1, 1)
+                nx = n - ends if dx else whole - 2 * ends
+                sx = near + {1: whole - n, -1: ends, 0: ends}[dx]
+                tx = {1: near - n, -1: near + whole + ends, 0: near + ends}[dx]
+                if nx > 0:
+                    send(
+                        ref.at[sx : sx + nx, sy : sy + ny], ref.at[tx : tx + nx, ty : ty + ny],
+                        which, device(dx, dy),
+                    )
+
+    for at in (5, 16):
+        fine_operator(at, 11)
+    inner = level_1(1, 10)
+    p1[7:17, 0:8, :] = packed_1(inner)
+    send_1(p1, 2, 6, 12, (5, 3, 1), 1)
+    groups[2] = p1.at[0:13]
+    sweep(b0, va0, 6, 25, 4, w0, b0, 1, 1)
+    arrived(11)
+    arrived(12)
+    fine_operator(1, 4)
+    fine_operator(27, 4)
+
+    lower, upper = level_1(0, 0), level_1(11, 11)
+    b1p[3:4, 0:8, :] = packed_1(lower)
+    b1p[8:9, 0:8, :] = packed_1(upper)
+    op1 = (
+        jnp.concatenate([lower[0][0:1], inner[0], upper[0][1:2]], axis=0),
+        *(jnp.concatenate(parts, axis=0) for parts in zip(lower[1:], inner[1:], upper[1:])),
+    )
+    s1[...] = damping / own_diagonal(op1, 2)
+
+    sweep(b0, va0, 2, 5, 4, w0, b0, 1, 1)
+    sweep(b0, va0, 26, 29, 4, w0, b0, 1, 1)
 
     def residual_0(index, carry):
         at = 4 + 6 * index
@@ -258,12 +283,12 @@
         r = pair_x(d0[pl.ds(at, 6)] * (total - here))
         r = pair(pair(r, 1, 1), 1, 2) * s1[pl.ds(3 * index, 3)]
         ybit, zbit = odd(r[0:1], 1, 1), odd(r[0:1], 1, 2)
-        b1p[pl.ds(2 + index, 1), 0:8, :] = jnp.where(zbit, jnp.where(ybit, r[2:3], r[1:2]), r[0:1])
+        b1p[pl.ds(4 + index, 1), 0:8, :] = jnp.where(zbit, jnp.where(ybit, r[2:3], r[1:2]), r[0:1])
         return carry
 
     lax.fori_loop(0, 4, residual_0, 0, unroll=True)
-    send_1(b1p, 3, 2, 4, (2, 1, 1))
-    groups[3] = b1p.at[0:6]
+    send_1(b1p, 3, 3, 6, (3, 3, 2), 0)
+    groups[3] = b1p.at[0:10]
 
     op2 = coarsen(op1, 2)
     px, py, _, pz, mass = op2
@@ -291,7 +316,7 @@
     def gather_plane(source, target, which):
         seat = core * 8 + chip_y
         target[:, pl.ds(seat, 1), :] = source[:, 0:1, :]
-        each(16, lambda k: send(source.at[:, 0:1], target.at[:, pl.ds(seat, 1)], which, in_plane(k)))
+        each(15, lambda k: send(source.at[:, 0:1], target.at[:, pl.ds(seat, 1)], which, in_plane(k)))
         groups[which] = target.at[:, 0:15]
 
     def merge(source, target, kinds):
@@ -306,34 +331,33 @@
         piece = source.at[kinds, :, :, 0:1]
         seat = target.at[kinds, half, :, pl.ds(gy % 4 // 2 * 2, 2), pl.ds(gy // 4, 1)]
         pltpu.make_async_copy(piece, seat, recv_sem.at[which]).start()
-        each(32, lambda k: send(piece, seat, which, in_column(k)))
+        each(31, lambda k: send(piece, seat, which, in_column(k)))
 
     gather_plane(o3, g1o, 6)
 
     arrived(2)
 
-    def weights_1(index, carry):
-        at = 1 + 2 * index
-        packed = p1[pl.ds(at - 1, 3)]
+    def weights_1(at, count):
+        packed = p1[at - 1 : at + count]
         even_z, odd_z = low(packed, 1, 2), high(packed[1:], 1, 2)
         px, pz = low(even_z, 1, 1), high(even_z[1:], 1, 1)
         py, mass = low(odd_z, 1, 1), high(odd_z, 1, 1)
-        diagonal, _ = normalise(px[1:], px[:-1], py, down(py, 2, 1), pz, down(pz, 2, 2), mass, w1, at, 2)
-        d1[pl.ds(at, 2)] = diagonal * (1.0 / damping)
-        return carry
-
-    lax.fori_loop(0, 11, weights_1, 0, unroll=True)
+        diagonal, _ = normalise(px[1:], px[:-1], py, down(py, 2, 1), pz, down(pz, 2, 2), mass, w1, at, count)
+        d1[at : at + count] = diagonal * (1.0 / damping)
+
+    for at, count in ((1, 4), (8, 3), (11, 3), (14, 3), (20, 3)):
+        weights_1(at, count)
     arrived(3)
-
-    def unpack_1(index, carry):
-        packed = b1p[pl.ds(index, 1)]
+    for plane, end in ((5, 2), (6, 3), (17, 8), (18, 9)):
+        p1[plane] = b1p[end]
+    for at in (5, 17):
+        weights_1(at, 3)
+    for index, plane in enumerate((0, 1, 4, 5, 6, 7, 10, 11)):
+        packed = b1p[plane : plane + 1]
         odd_z = high(packed, 1, 2)
-        b1[pl.ds(3 * index, 1)] = low(packed, 1, 2)
-        b1[pl.ds(3 * index + 1, 1)] = low(odd_z, 1, 1)
-        b1[pl.ds(3 * index + 2, 1)] = high(odd_z, 1, 1)
-        return carry
-
-    lax.fori_loop(0, 8, unpack_1, 0, unroll=True)
+        b1[3 * index : 3 * index + 1] = low(packed, 1, 2)
+        b1[3 * index + 1 : 3 * index + 2] = low(odd_z, 1, 1)
+        b1[3 * index + 2 : 3 * index + 3] = high(odd_z, 1, 1)
     sweep(b1, va1, 1, 22, 2, w1, b1, 2, 2)
 
     arrived(4)
@@ -455,14 +479,14 @@
     sweep(va2, vb2, 3, 14, 4, w2, b2, 1, 4)
     sweep(vb2, va2, 4, 13, 5, w2, b2, 1, 4)
 
-    upper = place((1, 8, BZ), 1) >= 4
+    second = place((1, 8, BZ), 1) >= 4
 
     def correct_1(index, carry):
         for rows, first in ((0, 0), (8, 2), (24, 14)):
             a = va2[pl.ds(4 + index, 1), first : first + 1, :]
             b = va2[pl.ds(4 + index, 1), first + 1 : first + 2, :]
             at = pl.ds(2 + 2 * index, 2)
-            va1[at, rows : rows + 8, :] = va1[at, rows : rows + 8, :] + jnp.where(upper, b, a)
+            va1[at, rows : rows + 8, :] = va1[at, rows : rows + 8, :] + jnp.where(second, b, a)
         return carry
 
     lax.fori_loop(0, 10, correct_1, 0, unroll=True)
@@ -473,24 +497,25 @@
         at = pl.ds(2 + 2 * index, 2)
         coarse = va1[pl.ds(5 + index, 1)]
         va0[at, 0:8, :] = va0[at, 0:8, :] + coarse[:, 0:8]
-        va0[at, 8:16, :] = va0[at, 8:16, :] + jnp.where(upper, coarse[:, 24:32], coarse[:, 8:16])
+        va0[at, 8:16, :] = va0[at, 8:16, :] + jnp.where(second, coarse[:, 24:32], coarse[:, 8:16])
         return carry
 
     lax.fori_loop(0, 14, correct_0, 0, unroll=True)
     sweep(va0, vb0, 2, 29, 4, w0, b0, 1, 1)
 
-    def finish(index, carry):
-        at = 4 + 4 * index
-        _, total = step(vb0, at, 4, w0, b0, 1, 1, 8)
-        out[pl.ds(4 * index, 4)] = total
-        return carry
-
-    lax.fori_loop(0, 6, finish, 0, unroll=True)
-
-    for which in (0, 1, 2, 3, 4, 5, 6, 8, 10):
+    results = []
+    for at in (0, 8, 16):
+        _, total = step(vb0, 4 + at, 8, w0, b0, 1, 1, 8)
+        obuf[at : at + 8] = total
+        results.append(pltpu.make_async_copy(obuf.at[at : at + 8], out.at[at : at + 8], local_sem.at[2 + at // 8]))
+        results[-1].start()
+
+    for which in (0, 1, 2, 3, 4, 5, 6, 8, 10, 11, 12):
         await_bytes(groups[which], send_sem.at[which])
     await_bytes(p1.at[0:12, 0:31], send_sem.at[7])
     await_bytes(p1.at[0:6, 0:31], send_sem.at[9])
+    for copy in results:
+        copy.wait()
 
 
 def shards(intensities, labels):
@@ -502,24 +527,24 @@
         kernel,
         out_shape=jax.ShapeDtypeStruct((BX, BY, BZ), f32),
         in_specs=[pl.BlockSpec(memory_space=pltpu.HBM)] * 2,
-        out_specs=pl.BlockSpec(memory_space=pltpu.VMEM),
+        out_specs=pl.BlockSpec(memory_space=pltpu.HBM),
         scratch_shapes=[
-            vmem(*zero, dtype=jnp.int32), vmem(*zero, dtype=jnp.int32),
+            vmem(*zero, dtype=jnp.int32), vmem(*zero, dtype=jnp.int32), vmem(BX, BY, BZ),
             [vmem(*zero)] * 6, vmem(*zero), vmem(32, 8, BZ), vmem(5, 32, 8, BZ),
             vmem(*zero), vmem(*zero),
-            vmem(*one), vmem(8, 32, BZ), vmem(*one), [vmem(*one)] * 6, vmem(*one), vmem(12, 8, BZ),
+            vmem(*one), vmem(12, 32, BZ), vmem(*one), [vmem(*one)] * 6, vmem(*one), vmem(12, 8, BZ),
             vmem(*one), vmem(*one),
             vmem(*two), vmem(*two), vmem(*two), [vmem(*two)] * 6, vmem(*two), vmem(*two),
             vmem(*two), vmem(*two),
             vmem(12, 8, BZ), vmem(12, 16, BZ), vmem(4, 3, 2, 8, BZ), vmem(4, 2, 3, 4, 8, BZ),
             vmem(3, 8, BZ), vmem(3, 16, BZ), vmem(1, 3, 2, 8, BZ), vmem(1, 2, 3, 4, 8, BZ),
             vmem(6, 3, 4, 2, 8, BZ), vmem(3, 4, 2, 8, BZ), vmem(3, 4, 2, 8, BZ),
-            pltpu.SemaphoreType.DMA((2,)),
-            pltpu.SemaphoreType.DMA((11,)),
-            pltpu.SemaphoreType.DMA((11,)),
+            pltpu.SemaphoreType.DMA((5,)),
+            pltpu.SemaphoreType.DMA((13,)),
+            pltpu.SemaphoreType.DMA((13,)),
         ],
         compiler_params=pltpu.CompilerParams(
-            collective_id=0, has_side_effects=True, vmem_limit_bytes=40 * 1024 * 1024
+            collective_id=0, has_side_effects=True, vmem_limit_bytes=64 * 1024 * 1024
         ),
         name="v_cycle",
     )(intensities, labels)

time: 52.9 us -> 51.4 us (0.972)
  local copies, waits for them, and re-layouts: 2.43 us -> 1.54 us
    unnamed x5 -> x1, local copies, waits for them, and re-layouts: 2.43 us -> 1.54 us
where the time goes in v3:
time: 51.4 us; the launch traced here: 51.3 us
  Pallas kernels  49.8 us (97%)
  local copies, waits for them, and re-layouts  1.54 us (3%)
    pallas_call x1, Pallas kernels, shards(): pl.pallas_call(kernel, out_shape=jax.ShapeDtypeStruct((BX, BY, BZ), f32),...  49.8 us
    unnamed x1, local copies, waits for them, and re-layouts  1.54 us

profile of v3, /device:TPU:1, one launch (start us, length us, event | category | flops | bytes accessed | tf_op | source)
XLA Modules:
  0.0 51.3 jit_solution(2917430367197577711)
XLA Ops:
  0.0 49.8 %v_cycle.1 = f32[24,8,128]{2,1,0:T(8,128)} custom-call(s32[24,8,128]{2,1,0:T(8,128)} %ints.1, s32[24,8,128]{2,1,0:T(8,128)} %labels.1), custom_call_target="tpu_custom_call" | custom-call | tf_op jit(solution)/shard_map/v_cycle/pallas_call | solution.py:526
  49.8 1.5 %copy.4 = f32[24,8,128]{2,1,0:T(8,128)} copy(f32[24,8,128]{2,1,0:T(8,128)} %v_cycle.1) | data formatting | bytes 196608

commit v4 on v3

--- a/solution.py
+++ b/solution.py
@@ -115,7 +115,7 @@
 
 def kernel(
     ints, labels, out,
-    ibuf, lbuf, obuf, w0, b0, d0, fine, va0, vb0,
+    ibuf, lbuf, w0, b0, d0, fine, va0, vb0,
     p1, b1p, b1, w1, d1, s1, va1, vb1,
     p2, x2, b2, w2, d2, s2, va2, vb2,
     o3, g1o, qo, g2o, o4, g1, q, g2, w3, b3, solved,
@@ -151,7 +151,7 @@
             action(index)
             return carry
 
-        lax.fori_loop(0, count, turn, 0)
+        lax.fori_loop(0, count, turn, 0, unroll=True)
 
     def await_bytes(ref, sem):
         pltpu.make_async_copy(ref, ref, sem).wait()
@@ -360,6 +360,22 @@
         b1[3 * index + 2 : 3 * index + 3] = high(odd_z, 1, 1)
     sweep(b1, va1, 1, 22, 2, w1, b1, 2, 2)
 
+    def residual_1(index, carry):
+        at = 2 + 4 * index
+        here, total = step(va1, at, 4, w1, b1, 2, 2)
+        r = pair_x(d1[pl.ds(at, 4)] * (total - here))
+        r = pair(pair(r, 2, 1), 2, 2)
+        mine, after, before = r[:, 0:8], r[:, 8:16], r[:, 24:32]
+        row = place(mine.shape, 1)
+        first = jnp.where(row < 2, jnp.where(row == 0, mine, up(mine, 3, 1)), jnp.where(row == 2, down(after, 2, 1), up(after, 1, 1)))
+        last = jnp.where(row == 7, down(before, 3, 1), up(before, 2, 1))
+        to = pl.ds(4 + 2 * index, 2)
+        b2[to, 0:8, :] = first
+        b2[to, 8:16, :] = last
+        return carry
+
+    lax.fori_loop(0, 5, residual_1, 0, unroll=True)
+
     arrived(4)
 
     def weights_2(index, carry):
@@ -374,22 +390,7 @@
         return carry
 
     lax.fori_loop(0, 4, weights_2, 0, unroll=True)
-
-    def residual_1(index, carry):
-        at = 2 + 4 * index
-        here, total = step(va1, at, 4, w1, b1, 2, 2)
-        r = pair_x(d1[pl.ds(at, 4)] * (total - here))
-        r = pair(pair(r, 2, 1), 2, 2)
-        mine, after, before = r[:, 0:8], r[:, 8:16], r[:, 24:32]
-        row = place(mine.shape, 1)
-        first = jnp.where(row < 2, jnp.where(row == 0, mine, up(mine, 3, 1)), jnp.where(row == 2, down(after, 2, 1), up(after, 1, 1)))
-        last = jnp.where(row == 7, down(before, 3, 1), up(before, 2, 1))
-        to = pl.ds(4 + 2 * index, 2)
-        b2[to, 0:8, :] = first * s2[to, 0:8, :]
-        b2[to, 8:16, :] = last * s2[to, 8:16, :]
-        return carry
-
-    lax.fori_loop(0, 5, residual_1, 0, unroll=True)
+    b2[4:14] = b2[4:14] * s2[4:14]
 
     sweep(b2, va2, 5, 12, 4, w2, b2, 1, 4)
     here, total = step(va2, 6, 6, w2, b2, 1, 4, 8)
@@ -503,19 +504,14 @@
     lax.fori_loop(0, 14, correct_0, 0, unroll=True)
     sweep(va0, vb0, 2, 29, 4, w0, b0, 1, 1)
 
-    results = []
     for at in (0, 8, 16):
         _, total = step(vb0, 4 + at, 8, w0, b0, 1, 1, 8)
-        obuf[at : at + 8] = total
-        results.append(pltpu.make_async_copy(obuf.at[at : at + 8], out.at[at : at + 8], local_sem.at[2 + at // 8]))
-        results[-1].start()
+        out[at : at + 8] = total
 
     for which in (0, 1, 2, 3, 4, 5, 6, 8, 10, 11, 12):
         await_bytes(groups[which], send_sem.at[which])
     await_bytes(p1.at[0:12, 0:31], send_sem.at[7])
     await_bytes(p1.at[0:6, 0:31], send_sem.at[9])
-    for copy in results:
-        copy.wait()
 
 
 def shards(intensities, labels):
@@ -527,9 +523,9 @@
         kernel,
         out_shape=jax.ShapeDtypeStruct((BX, BY, BZ), f32),
         in_specs=[pl.BlockSpec(memory_space=pltpu.HBM)] * 2,
-        out_specs=pl.BlockSpec(memory_space=pltpu.HBM),
+        out_specs=pl.BlockSpec(memory_space=pltpu.VMEM),
         scratch_shapes=[
-            vmem(*zero, dtype=jnp.int32), vmem(*zero, dtype=jnp.int32), vmem(BX, BY, BZ),
+            vmem(*zero, dtype=jnp.int32), vmem(*zero, dtype=jnp.int32),
             [vmem(*zero)] * 6, vmem(*zero), vmem(32, 8, BZ), vmem(5, 32, 8, BZ),
             vmem(*zero), vmem(*zero),
             vmem(*one), vmem(12, 32, BZ), vmem(*one), [vmem(*one)] * 6, vmem(*one), vmem(12, 8, BZ),
@@ -539,12 +535,12 @@
             vmem(12, 8, BZ), vmem(12, 16, BZ), vmem(4, 3, 2, 8, BZ), vmem(4, 2, 3, 4, 8, BZ),
             vmem(3, 8, BZ), vmem(3, 16, BZ), vmem(1, 3, 2, 8, BZ), vmem(1, 2, 3, 4, 8, BZ),
             vmem(6, 3, 4, 2, 8, BZ), vmem(3, 4, 2, 8, BZ), vmem(3, 4, 2, 8, BZ),
-            pltpu.SemaphoreType.DMA((5,)),
+            pltpu.SemaphoreType.DMA((2,)),
             pltpu.SemaphoreType.DMA((13,)),
             pltpu.SemaphoreType.DMA((13,)),
         ],
         compiler_params=pltpu.CompilerParams(
-            collective_id=0, has_side_effects=True, vmem_limit_bytes=64 * 1024 * 1024
+            collective_id=0, has_side_effects=True, vmem_limit_bytes=55125 * 1024
         ),
         name="v_cycle",
     )(intensities, labels)

time: 51.4 us -> 48.4 us (0.942)
  Pallas kernels: 49.8 us -> 47.7 us
  local copies, waits for them, and re-layouts: 1.54 us -> 0.64 us
    pallas_call x1, Pallas kernels: 49.8 us -> 47.7 us  [shards(): pl.pallas_call(kernel, out_shape=jax.ShapeDtypeStruct((BX, BY, BZ), f32),...]
    unnamed x1, local copies, waits for them, and re-layouts: 1.54 us -> 0.64 us
where the time goes in v4:
time: 48.4 us; the launch traced here: 48.3 us
  Pallas kernels  47.7 us (99%)
  local copies, waits for them, and re-layouts  0.64 us (1%)
    pallas_call x1, Pallas kernels, shards(): pl.pallas_call(kernel, out_shape=jax.ShapeDtypeStruct((BX, BY, BZ), f32),...  47.7 us

profile of v4, /device:TPU:1, one launch (start us, length us, event | category | flops | bytes accessed | tf_op | source)
XLA Modules:
  0.0 48.3 jit_solution(7502934384125143362)
XLA Ops:
  0.0 47.7 %v_cycle.1 = f32[24,8,128]{2,1,0:T(8,128)S(1)} custom-call(s32[24,8,128]{2,1,0:T(8,128)} %ints.1, s32[24,8,128]{2,1,0:T(8,128)} %labels.1), custom_call_target="tpu_custom_call" | custom-call | tf_op jit(solution)/shard_map/v_cycle/pallas_call | solution.py:522
  47.7 0.6 %copy.4 = f32[24,8,128]{2,1,0:T(8,128)} copy(f32[24,8,128]{2,1,0:T(8,128)S(1)} %v_cycle.1) | data formatting | bytes 196608

commit v5 on v4

--- a/solution.py
+++ b/solution.py
@@ -305,8 +305,6 @@
             send(ref.at[sx : sx + n, 0:2], ref.at[tx : tx + n, ty : ty + 2], which, device(dx, dy))
         groups[which] = ref.at[0:7]
 
-    send_2(p2, 4)
-
     op3 = coarsen(op2, 4)
     s3 = damping / own_diagonal(op3, 8)
     px, py, _, pz, mass = op3
@@ -334,6 +332,7 @@
         each(31, lambda k: send(piece, seat, which, in_column(k)))
 
     gather_plane(o3, g1o, 6)
+    send_2(p2, 4)
 
     arrived(2)
 
@@ -347,6 +346,11 @@
 
     for at, count in ((1, 4), (8, 3), (11, 3), (14, 3), (20, 3)):
         weights_1(at, count)
+    arrived(6)
+    merge(g1o, qo, 4)
+    half_kinds = pl.ds(2 * core, 2)
+    gather_column(qo, g2o, 7, half_kinds)
+    groups[7] = g2o.at[0:2]
     arrived(3)
     for plane, end in ((5, 2), (6, 3), (17, 8), (18, 9)):
         p1[plane] = b1p[end]
@@ -399,11 +403,6 @@
     o4[...] = r * s3
     gather_plane(o4, g1, 8)
 
-    arrived(6)
-    merge(g1o, qo, 4)
-    half_kinds = pl.ds(2 * core, 2)
-    gather_column(qo, g2o, 7, half_kinds)
-    groups[7] = g2o.at[0:2]
     zbit = odd(here[:, 0:2], 1, 2)
     x2[6:12, 0:2, :] = jnp.where(zbit, b2[6:12, 0:2, :], here[:, 0:2])
     send_2(x2, 5)

time: 48.4 us -> 46.2 us (0.955)
  Pallas kernels: 47.7 us -> 45.5 us
    pallas_call x1, Pallas kernels: 47.7 us -> 45.5 us  [shards(): pl.pallas_call(kernel, out_shape=jax.ShapeDtypeStruct((BX, BY, BZ), f32),...]
where the time goes in v5:
time: 46.2 us; the launch traced here: 46.1 us
  Pallas kernels  45.5 us (98%)
  local copies, waits for them, and re-layouts  0.64 us (1%)
    pallas_call x1, Pallas kernels, shards(): pl.pallas_call(kernel, out_shape=jax.ShapeDtypeStruct((BX, BY, BZ), f32),...  45.5 us

profile of v5, /device:TPU:1, one launch (start us, length us, event | category | flops | bytes accessed | tf_op | source)
XLA Modules:
  0.0 46.1 jit_solution(12364090700565442937)
XLA Ops:
  0.0 45.5 %v_cycle.1 = f32[24,8,128]{2,1,0:T(8,128)S(1)} custom-call(s32[24,8,128]{2,1,0:T(8,128)} %ints.1, s32[24,8,128]{2,1,0:T(8,128)} %labels.1), custom_call_target="tpu_custom_call" | custom-call | tf_op jit(solution)/shard_map/v_cycle/pallas_call | solution.py:521
  45.5 0.6 %copy.4 = f32[24,8,128]{2,1,0:T(8,128)} copy(f32[24,8,128]{2,1,0:T(8,128)S(1)} %v_cycle.1) | data formatting | bytes 196608

commit v6 on v5

--- a/solution.py
+++ b/solution.py
@@ -172,8 +172,8 @@
 
     for dx, dy in MIDDLE:
         greet(device(dx, dy))
+    each(15, lambda k: greet(in_plane(k)))
     each(31, lambda k: greet(in_column(k)))
-    each(15, lambda k: greet(in_plane(k)))
     p2[:, 6:12, :] = jnp.ones((18, 6, BZ), f32)
     x2[:, 6:12, :] = jnp.zeros((18, 6, BZ), f32)
     pl.semaphore_wait(barrier, len(MIDDLE) + 15 + 31)
@@ -260,36 +260,41 @@
     send_1(p1, 2, 6, 12, (5, 3, 1), 1)
     groups[2] = p1.at[0:13]
     sweep(b0, va0, 6, 25, 4, w0, b0, 1, 1)
-    arrived(11)
-    arrived(12)
-    fine_operator(1, 4)
-    fine_operator(27, 4)
-
-    lower, upper = level_1(0, 0), level_1(11, 11)
-    b1p[3:4, 0:8, :] = packed_1(lower)
-    b1p[8:9, 0:8, :] = packed_1(upper)
-    op1 = (
-        jnp.concatenate([lower[0][0:1], inner[0], upper[0][1:2]], axis=0),
-        *(jnp.concatenate(parts, axis=0) for parts in zip(lower[1:], inner[1:], upper[1:])),
-    )
-    s1[...] = damping / own_diagonal(op1, 2)
-
-    sweep(b0, va0, 2, 5, 4, w0, b0, 1, 1)
-    sweep(b0, va0, 26, 29, 4, w0, b0, 1, 1)
-
-    def residual_0(index, carry):
+    s1[1:11] = damping / own_diagonal(inner, 2)
+
+    def residual_0(index):
         at = 4 + 6 * index
         here, total = step(va0, at, 6, w0, b0, 1, 1, 8)
         r = pair_x(d0[pl.ds(at, 6)] * (total - here))
         r = pair(pair(r, 1, 1), 1, 2) * s1[pl.ds(3 * index, 3)]
         ybit, zbit = odd(r[0:1], 1, 1), odd(r[0:1], 1, 2)
         b1p[pl.ds(4 + index, 1), 0:8, :] = jnp.where(zbit, jnp.where(ybit, r[2:3], r[1:2]), r[0:1])
-        return carry
-
-    lax.fori_loop(0, 4, residual_0, 0, unroll=True)
+
+    residual_0(1)
+    residual_0(2)
+    arrived(11)
+    arrived(12)
+    fine_operator(1, 4)
+    fine_operator(27, 4)
+
+    lower, upper = level_1(0, 0), level_1(11, 11)
+    b1p[3:4, 0:8, :] = packed_1(lower)
+    b1p[8:9, 0:8, :] = packed_1(upper)
+    s1[0:1] = damping / own_diagonal(lower, 2)
+    s1[11:12] = damping / own_diagonal(upper, 2)
+
+    sweep(b0, va0, 2, 5, 4, w0, b0, 1, 1)
+    sweep(b0, va0, 26, 29, 4, w0, b0, 1, 1)
+
+    residual_0(0)
+    residual_0(3)
     send_1(b1p, 3, 3, 6, (3, 3, 2), 0)
     groups[3] = b1p.at[0:10]
 
+    op1 = (
+        jnp.concatenate([lower[0][0:1], inner[0], upper[0][1:2]], axis=0),
+        *(jnp.concatenate(parts, axis=0) for parts in zip(lower[1:], inner[1:], upper[1:])),
+    )
     op2 = coarsen(op1, 2)
     px, py, _, pz, mass = op2
     slot = place(py.shape, 2) % 4
@@ -328,8 +333,8 @@
     def gather_column(source, target, which, kinds):
         piece = source.at[kinds, :, :, 0:1]
         seat = target.at[kinds, half, :, pl.ds(gy % 4 // 2 * 2, 2), pl.ds(gy // 4, 1)]
+        each(31, lambda k: send(piece, seat, which, in_column(k)))
         pltpu.make_async_copy(piece, seat, recv_sem.at[which]).start()
-        each(31, lambda k: send(piece, seat, which, in_column(k)))
 
     gather_plane(o3, g1o, 6)
     send_2(p2, 4)

time: 46.2 us -> 45.8 us (level)
  Pallas kernels: 45.5 us -> 45 us
where the time goes in v6:
time: 45.8 us; the launch traced here: 45.7 us
  Pallas kernels  45 us (98%)
  local copies, waits for them, and re-layouts  0.64 us (1%)
    pallas_call x1, Pallas kernels, shards(): pl.pallas_call(kernel, out_shape=jax.ShapeDtypeStruct((BX, BY, BZ), f32),...  45 us

profile of v6, /device:TPU:1, one launch (start us, length us, event | category | flops | bytes accessed | tf_op | source)
XLA Modules:
  0.0 45.7 jit_solution(15117370519828904664)
XLA Ops:
  0.0 45.0 %v_cycle.1 = f32[24,8,128]{2,1,0:T(8,128)S(1)} custom-call(s32[24,8,128]{2,1,0:T(8,128)} %ints.1, s32[24,8,128]{2,1,0:T(8,128)} %labels.1), custom_call_target="tpu_custom_call" | custom-call | tf_op jit(solution)/shard_map/v_cycle/pallas_call | solution.py:526
  45.0 0.6 %copy.4 = f32[24,8,128]{2,1,0:T(8,128)} copy(f32[24,8,128]{2,1,0:T(8,128)S(1)} %v_cycle.1) | data formatting | bytes 196608
